TPU v7x, 32 devices: a whole 2x2x4 slice. The times are simulated.
32 devices in a mesh: fsdp: 4 (over y, core), ctx: 2 (over x), tp: 4 (over z).
Axes of the slice: x: 2, y: 2, z: 4, core: 2. Of those that a mesh axis runs over, the one named last changes fastest.
Arguments:
- hidden_in: bfloat16 [1024, 16, 768], P(('ctx', 'tp'), 'fsdp'), may hold values from -6 to 6
- rand_blocks: int32 [16, 16, 12, 3], P('fsdp', None, 'tp'), may hold values from 0 to 15, as said below
- w_in: float32 [768, 12, 192], P('fsdp', 'tp'), may hold values from -0.21875 to 0.21875
- qv_bias: float32 [2, 768], P(None, ('tp', 'fsdp')), may hold values from -1.2 to 1.2
- w_out: float32 [768, 768], P('tp', 'fsdp'), may hold values from -1.75 to 1.75
- out_bias: float32 [2, 768], P(None, 'fsdp'), may hold values from -3 to 3
- norm_gain: float32 [2, 768], P(None, 'fsdp'), may hold values from 0.1 to 1.9
- norm_bias: float32 [2, 768], P(None, 'fsdp'), may hold values from -3 to 3
- w_up: float32 [768, 3072], P('fsdp', 'tp'), may hold values from -0.21875 to 0.21875
- up_bias: float32 [3072], P(('tp', 'fsdp')), may hold values from -3 to 3
- w_down: float32 [3072, 768], P('tp', 'fsdp'), may hold values from -0.15625 to 0.15625
- cotangent: bfloat16 [1024, 16, 768], P(('ctx', 'tp'), 'fsdp'), may hold values from -6 to 6
Outputs:
- layer_out: bfloat16 [1024, 16, 768], P(('ctx', 'tp'), 'fsdp')
- grad_in: bfloat16 [1024, 16, 768], P(('ctx', 'tp'), 'fsdp')
- grad_w_in: float32 [768, 12, 192], P('fsdp', 'tp')
- grad_qv_bias: float32 [2, 768], P(None, ('tp', 'fsdp'))
- grad_w_out: float32 [768, 768], P('tp', 'fsdp')
- grad_out_bias: float32 [2, 768], P(None, 'fsdp')
- grad_norm_gain: float32 [2, 768], P(None, 'fsdp')
- grad_norm_bias: float32 [2, 768], P(None, 'fsdp')
- grad_w_up: float32 [768, 3072], P('fsdp', 'tp')
- grad_up_bias: float32 [3072], P(('tp', 'fsdp'))
- grad_w_down: float32 [3072, 768], P('tp', 'fsdp')
Inputs may be any that keep to these rules, and one draw needn't show every extreme that they name: `rand_blocks`: for each sequence, head, pick and position p in 0..7 there is one k such that the random block of query block b = j * 8 + p lies in blocks ((j + k) mod (2)) * 8 to that plus 8 - 1, for every j. Over the 4 sequences of one index of fsdp, the heads of one index of tp, the picks and the positions, every k in 0..1 is taken equally often.
All inputs are finite; a program needn't handle non-finite values.
Results may differ from a plain program's by a relative error of at most 0.015.
The roundings to bfloat16 on the way count: a program that leaves them out, or rounds other values in their place, can miss the bound.
Values may be sent and summed in bfloat16 or wider, within the bound.
A program may use at most 192 MiB of HBM per device.

v0:
```python
import jax
import jax.numpy as jnp
from jax import lax
from jax.sharding import PartitionSpec as P

BLK = 64


EPS = 1e-06
NEG = -1000000000.0


def from_root(block, axis, owner):
    block = jnp.where(lax.axis_index(axis) == owner, block, jnp.zeros_like(block))
    return lax.psum(block, axis)


def extended(array, sides, width):
    for axis, dim in sides:
        size, length = (lax.axis_size(axis), array.shape[dim])
        up = [(i, (i + 1) % size) for i in range(size - 1)]
        down = [(j, i) for i, j in up]
        last = lax.slice_in_dim(array, length - width, length, axis=dim)
        leading = lax.slice_in_dim(array, 0, width, axis=dim)
        before = lax.ppermute(last, axis, up)
        after = lax.ppermute(leading, axis, down)
        array = jnp.concatenate([before, array, after], axis=dim)
    return array


def joined_2(part, axis, combine):
    gathered = jax.tree.map(lambda a: lax.all_gather(a, axis), part)

    def take(source):
        return jax.tree.map(lambda a: lax.dynamic_index_in_dim(a, source, 0, False), gathered)

    return lax.fori_loop(
        1, lax.axis_size(axis), lambda source, state: combine(state, take(source)), take(0)
    )


def norm_forward(value, gain, shift):
    mean = jnp.mean(value, axis=-1, keepdims=True)
    centred = value - mean
    inverse = lax.rsqrt(jnp.mean(centred * centred, axis=-1, keepdims=True) + EPS)
    normed = centred * inverse
    return (normed * gain + shift, normed, inverse)


def norm_backward(upper, normed, inverse, gain):
    scaled = upper * gain
    return inverse * (
        scaled
        - jnp.mean(scaled, axis=-1, keepdims=True)
        - normed * jnp.mean(scaled * normed, axis=-1, keepdims=True)
    )


def exact_gelu(value):
    return jax.nn.gelu(value, approximate=False)


def outer_sum(left, right):
    return lax.dot_general(
        left, right, (((0,), (0,)), ((), ())), preferred_element_type=jnp.float32
    )


def rows_all(value):
    return lax.all_gather(value, "tp", axis=0, tiled=True)


def rows_sum(left, right, contract):
    return lax.psum_scatter(
        lax.dot_general(
            left, right, (((1,), (contract,)), ((), ())), preferred_element_type=jnp.float32
        ),
        "tp",
        scatter_dimension=0,
        tiled=True,
    )


def spread(piece, root):
    return from_root(piece, "ctx", root)


def stats_join(first_stats, second_stats):
    top = jnp.maximum(first_stats[0], second_stats[0])
    total = first_stats[1] * jnp.exp(first_stats[0] - top) + second_stats[1] * jnp.exp(
        second_stats[0] - top
    )
    return (top, total)


def split_groups(array, steps, group):
    return array.reshape((steps, group) + array.shape[1:])


def key_set(window_pad, global_pair, random_pairs):
    per_dev = random_pairs.shape[3]
    window = jnp.stack(
        [window_pad[:, :, offset_by : offset_by + per_dev] for offset_by in range(3)], axis=3
    )
    target_shape = global_pair.shape[:2] + (per_dev,) + global_pair.shape[2:]
    global_all = jnp.broadcast_to(global_pair[:, :, None], target_shape)
    random_all = jnp.swapaxes(random_pairs, 2, 3)
    joined = jnp.concatenate([window, global_all, random_all], axis=3)
    shape = joined.shape
    return joined.reshape(shape[0], shape[1], shape[2], shape[3] * shape[4], shape[5])


def scores_of(query, keys, mask, scale):
    head_dim = query.shape[-1]
    raw = (
        jnp.einsum(
            "shpqd,shpkd->shpqk", query, keys[..., :head_dim], preferred_element_type=jnp.float32
        )
        * scale
    )
    return jnp.where(mask, raw, NEG)


def attend_group(query, window_pad, global_pair, random_pairs, mask, scale):
    head_dim = query.shape[-1]
    keys = key_set(window_pad, global_pair, random_pairs)
    scores = scores_of(query, keys, mask, scale)
    top = jnp.max(scores, axis=-1, keepdims=True)
    weights = jnp.exp(scores - top)
    total = jnp.sum(weights, axis=-1, keepdims=True)
    probs = (weights / total).astype(jnp.bfloat16)
    mixed = jnp.einsum(
        "shpqk,shpkd->shpqd", probs, keys[..., head_dim:], preferred_element_type=jnp.float32
    )
    return (mixed.astype(jnp.bfloat16), (top + jnp.log(total))[..., 0])


def attend_back(query, window_pad, global_pair, random_pairs, mask, scale, logsum, mixed_grad):
    head_dim = query.shape[-1]
    blocksize = window_pad.shape[3]
    keys = key_set(window_pad, global_pair, random_pairs)
    scores = scores_of(query, keys, mask, scale)
    probs = jnp.exp(scores - logsum[..., None])
    probs_grad = jnp.einsum(
        "shpqd,shpkd->shpqk", mixed_grad, keys[..., head_dim:], preferred_element_type=jnp.float32
    )
    inner = jnp.sum(probs * probs_grad, axis=-1, keepdims=True)
    scores_grad = (probs * (probs_grad - inner)).astype(jnp.bfloat16)
    query_grad = (
        jnp.einsum(
            "shpqk,shpkd->shpqd",
            scores_grad,
            keys[..., :head_dim],
            preferred_element_type=jnp.float32,
        )
        * scale
    )
    keys_grad = (
        jnp.einsum("shpqk,shpqd->shpkd", scores_grad, query, preferred_element_type=jnp.float32)
        * scale
    )
    values_grad = jnp.einsum(
        "shpqk,shpqd->shpkd",
        probs.astype(jnp.bfloat16),
        mixed_grad,
        preferred_element_type=jnp.float32,
    )
    pairs_grad = jnp.concatenate([keys_grad, values_grad], axis=-1)
    shape = pairs_grad.shape
    pairs_grad = pairs_grad.reshape(
        shape[0], shape[1], shape[2], shape[3] // blocksize, blocksize, shape[4]
    )
    per_dev = shape[2]
    window_grad = jnp.zeros(window_pad.shape, jnp.float32)
    for offset_by in range(3):
        window_grad = window_grad.at[:, :, offset_by : offset_by + per_dev].add(
            pairs_grad[:, :, :, offset_by]
        )
    global_grad = jnp.sum(pairs_grad[:, :, :, 3:5], axis=2)
    random_grad = jnp.swapaxes(pairs_grad[:, :, :, 5:], 2, 3)
    return (query_grad, window_grad, global_grad, random_grad)


def shards(
    hidden_in,
    rand_blocks,
    w_in,
    qv_bias,
    w_out,
    out_bias,
    norm_gain,
    norm_bias,
    w_up,
    up_bias,
    w_down,
    cotangent,
):
    ctx_count = lax.axis_size("ctx")
    tp_count = lax.axis_size("tp")
    ctx_place = lax.axis_index("ctx")
    part_rows, seqs, width = hidden_in.shape
    heads = w_in.shape[1]
    head_dim = w_in.shape[2] // 3
    pair_width = 2 * head_dim
    blocks_all = rand_blocks.shape[1]
    picks = rand_blocks.shape[3]
    length = part_rows * tp_count
    per_dev = length // BLK
    total_rows = length * seqs
    scale = head_dim ** (-0.5)
    group = min(seqs, max(1, 512 // length))
    steps = seqs // group
    first_owner = ctx_place == 0
    last_owner = ctx_place == ctx_count - 1
    gathered = (
        lax.all_gather(w_in.astype(jnp.bfloat16), "fsdp", axis=0, tiled=True),
        lax.all_gather(qv_bias.astype(jnp.bfloat16), "fsdp", axis=1, tiled=True),
        lax.all_gather(w_out.astype(jnp.bfloat16), "fsdp", axis=1, tiled=True),
        lax.all_gather(out_bias.astype(jnp.bfloat16), "fsdp", axis=1, tiled=True),
        lax.all_gather(norm_gain.astype(jnp.bfloat16), "fsdp", axis=1, tiled=True),
        lax.all_gather(norm_bias.astype(jnp.bfloat16), "fsdp", axis=1, tiled=True),
        lax.all_gather(w_up.astype(jnp.bfloat16), "fsdp", axis=0, tiled=True),
        lax.all_gather(up_bias.astype(jnp.bfloat16), "fsdp", axis=0, tiled=True),
        lax.all_gather(w_down.astype(jnp.bfloat16), "fsdp", axis=1, tiled=True),
    )
    input_low = gathered[0].reshape(width, heads * 3 * head_dim)
    bias_pair = gathered[1].astype(jnp.float32).reshape(2, heads, head_dim)
    output_low = gathered[2]
    bias_out = gathered[3].astype(jnp.float32)
    gains = gathered[4].astype(jnp.float32)
    shifts = gathered[5].astype(jnp.float32)
    upper_low = gathered[6]
    bias_up = gathered[7].astype(jnp.float32)
    lower_low = gathered[8]
    x_full = rows_all(hidden_in)
    x_rows = x_full.reshape(total_rows, width)
    projected = jnp.dot(x_rows, input_low, preferred_element_type=jnp.float32).reshape(
        length, seqs, heads, 3, head_dim
    )
    query = (projected[:, :, :, 0] + bias_pair[0]).astype(jnp.bfloat16)
    key = projected[:, :, :, 1].astype(jnp.bfloat16)
    value = (projected[:, :, :, 2] + bias_pair[1]).astype(jnp.bfloat16)
    query_heads = query.transpose(1, 2, 0, 3).reshape(seqs, heads, per_dev, BLK, head_dim)
    pairs = jnp.concatenate([key, value], axis=-1).transpose(1, 2, 0, 3)
    window_pad = extended(pairs, (("ctx", 2),), BLK).reshape(
        seqs, heads, per_dev + 2, BLK, pair_width
    )
    pair_blocks = pairs.reshape(seqs, heads, per_dev, BLK, pair_width)
    triple_blocks = jnp.concatenate([query_heads, pair_blocks], axis=-1)
    global_triple = jnp.stack(
        [
            spread(triple_blocks[:, :, 0], 0),
            spread(triple_blocks[:, :, per_dev - 1], ctx_count - 1),
        ],
        axis=2,
    )
    global_query = global_triple[..., :head_dim]
    global_pair = global_triple[..., head_dim:]
    key_local = pairs[..., :head_dim]
    value_local = pairs[..., head_dim:]
    wide_scores = (
        jnp.einsum("shgqd,shkd->shgqk", global_query, key_local, preferred_element_type=jnp.float32)
        * scale
    )
    wide_top = jnp.max(wide_scores, axis=-1)
    wide_total = jnp.sum(jnp.exp(wide_scores - wide_top[..., None]), axis=-1)
    all_top, all_total = joined_2((wide_top, wide_total), "ctx", stats_join)
    wide_probs = jnp.exp(wide_scores - (all_top + jnp.log(all_total))[..., None])
    wide_probs_low = wide_probs.astype(jnp.bfloat16)
    mix_low = jnp.einsum(
        "shgqk,shkd->shgqd", wide_probs_low, value_local, preferred_element_type=jnp.float32
    )
    mix_full = jnp.einsum(
        "shgqk,shkd->shgqd",
        wide_probs,
        value_local.astype(jnp.float32),
        precision=lax.Precision.HIGHEST,
    )
    mix_low, mix_full = lax.psum((mix_low, mix_full), "ctx")
    global_mixed = mix_low.astype(jnp.bfloat16)
    units = seqs * heads * picks * per_dev
    table = rand_blocks.transpose(0, 2, 3, 1).reshape(seqs, heads, picks, ctx_count, per_dev)
    table = table.transpose(0, 1, 2, 4, 3).reshape(units, ctx_count)
    mine = lax.dynamic_index_in_dim(table, ctx_place, 1, keepdims=False)
    mine_groups = mine.reshape(steps, group, heads, picks, per_dev)
    seq_pick = jnp.arange(group)[:, None, None, None]
    head_pick = jnp.arange(heads)[None, :, None, None]
    block_index = ctx_place * per_dev + jnp.arange(per_dev)
    present = jnp.concatenate(
        [
            (block_index >= 1)[:, None],
            jnp.ones((per_dev, 1), jnp.bool_),
            (block_index <= blocks_all - 2)[:, None],
            jnp.ones((per_dev, 2 + picks), jnp.bool_),
        ],
        axis=1,
    )
    mask = jnp.repeat(present, BLK, axis=1)[None, None, :, None, :]

    def random_pairs_for(block_group, id_group):
        whole = lax.all_gather(block_group, "ctx", axis=2, tiled=True)
        return whole[seq_pick, head_pick, id_group]

    query_groups = split_groups(query_heads, steps, group)
    pad_groups = split_groups(window_pad, steps, group)
    global_groups = split_groups(global_pair, steps, group)
    block_groups = split_groups(pair_blocks, steps, group)

    def forward_step(items):
        position, query_group, pad_group, global_group, block_group, id_group = items
        random_group = random_pairs_for(block_group, id_group)
        return attend_group(query_group, pad_group, global_group, random_group, mask, scale)

    mixed_groups, logsum_groups = lax.map(
        forward_step,
        (jnp.arange(steps), query_groups, pad_groups, global_groups, block_groups, mine_groups),
    )
    mixed_blocks = mixed_groups.reshape(seqs, heads, per_dev, BLK, head_dim)
    mixed_blocks = mixed_blocks.at[:, :, 0].set(
        jnp.where(first_owner, global_mixed[:, :, 0], mixed_blocks[:, :, 0])
    )
    mixed_blocks = mixed_blocks.at[:, :, per_dev - 1].set(
        jnp.where(last_owner, global_mixed[:, :, 1], mixed_blocks[:, :, per_dev - 1])
    )
    mixed = (
        mixed_blocks.reshape(seqs, heads, length, head_dim)
        .transpose(2, 0, 1, 3)
        .reshape(total_rows, heads * head_dim)
    )
    branch = rows_sum(mixed, output_low, 0) + bias_out[0]
    residual_in = hidden_in.reshape(part_rows * seqs, width).astype(jnp.float32)
    first, normed_one, inverse_one = norm_forward(residual_in + branch, gains[0], shifts[0])
    first_full = rows_all(first.astype(jnp.bfloat16).reshape(part_rows, seqs, width)).reshape(
        total_rows, width
    )
    inner = jnp.dot(first_full, upper_low, preferred_element_type=jnp.float32) + bias_up
    active_value, gelu_back = jax.vjp(exact_gelu, inner)
    active = active_value.astype(jnp.bfloat16)
    second = rows_sum(active, lower_low, 0) + bias_out[1]
    result, normed_two, inverse_two = norm_forward(first + second, gains[1], shifts[1])
    layer_out = result.astype(jnp.bfloat16).reshape(part_rows, seqs, width)
    upstream = cotangent.reshape(part_rows * seqs, width).astype(jnp.float32)
    second_grad = norm_backward(upstream, normed_two, inverse_two, gains[1])
    second_low = second_grad.astype(jnp.bfloat16)
    second_full = rows_all(second_low.reshape(part_rows, seqs, width)).reshape(total_rows, width)
    active_grad = lax.dot_general(
        second_full, lower_low, (((1,), (1,)), ((), ())), preferred_element_type=jnp.float32
    )
    inner_low = gelu_back(active_grad)[0].astype(jnp.bfloat16)
    first_grad = second_grad + rows_sum(inner_low, upper_low, 1)
    residual_grad = norm_backward(first_grad, normed_one, inverse_one, gains[0])
    branch_low = residual_grad.astype(jnp.bfloat16)
    branch_full = rows_all(branch_low.reshape(part_rows, seqs, width)).reshape(total_rows, width)
    mixed_grad = lax.dot_general(
        branch_full, output_low, (((1,), (1,)), ((), ())), preferred_element_type=jnp.float32
    ).astype(jnp.bfloat16)
    mixed_heads = (
        mixed_grad.reshape(length, seqs, heads, head_dim)
        .transpose(1, 2, 0, 3)
        .reshape(seqs, heads, per_dev, BLK, head_dim)
    )
    zero_block = jnp.zeros((seqs, heads, BLK, head_dim), jnp.bfloat16)
    lead_grad = jnp.where(first_owner, mixed_heads[:, :, 0], zero_block).astype(jnp.float32)
    tail_grad = jnp.where(last_owner, mixed_heads[:, :, per_dev - 1], zero_block).astype(
        jnp.float32
    )
    lead_sum, tail_sum = (
        lax.psum(lead_grad.astype(jnp.bfloat16), "ctx").astype(jnp.float32),
        lax.psum(tail_grad.astype(jnp.bfloat16), "ctx").astype(jnp.float32),
    )
    wide_grad = jnp.stack([lead_sum, tail_sum], axis=2).astype(jnp.bfloat16)
    mixed_heads = mixed_heads.at[:, :, 0].set(
        jnp.where(first_owner, zero_block, mixed_heads[:, :, 0])
    )
    mixed_heads = mixed_heads.at[:, :, per_dev - 1].set(
        jnp.where(last_owner, zero_block, mixed_heads[:, :, per_dev - 1])
    )

    def random_back(random_grad, id_group):
        spread_grad = (
            jnp.zeros((group, heads, blocks_all, BLK, pair_width), jnp.float32)
            .at[seq_pick, head_pick, id_group]
            .add(random_grad)
        )
        return lax.psum_scatter(
            spread_grad.astype(jnp.bfloat16), "ctx", scatter_dimension=2, tiled=True
        ).astype(jnp.float32)

    def backward_step(items):
        (
            position,
            query_group,
            pad_group,
            global_group,
            block_group,
            id_group,
            logsum_group,
            grad_group,
        ) = items
        random_group = random_pairs_for(block_group, id_group)
        query_grad, window_grad, global_grad, random_grad = attend_back(
            query_group,
            pad_group,
            global_group,
            random_group,
            mask,
            scale,
            logsum_group,
            grad_group,
        )
        return (query_grad, window_grad, global_grad, random_back(random_grad, id_group))

    query_grads, window_grads, global_grads, random_total = lax.map(
        backward_step,
        (
            jnp.arange(steps),
            query_groups,
            pad_groups,
            global_groups,
            block_groups,
            mine_groups,
            logsum_groups,
            split_groups(mixed_heads, steps, group),
        ),
    )
    query_grads = query_grads.reshape(seqs, heads, length, head_dim)
    window_grads = window_grads.reshape(seqs, heads, per_dev + 2, BLK, pair_width)
    global_grads = global_grads.reshape(seqs, heads, 2, BLK, pair_width)
    wide_inner = jnp.sum(wide_grad.astype(jnp.float32) * mix_full, axis=-1, keepdims=True)
    wide_probs_grad = jnp.einsum(
        "shgqd,shkd->shgqk", wide_grad, value_local, preferred_element_type=jnp.float32
    )
    wide_scores_grad = (wide_probs * (wide_probs_grad - wide_inner)).astype(jnp.bfloat16)
    wide_query_part = (
        jnp.einsum(
            "shgqk,shkd->shgqd", wide_scores_grad, key_local, preferred_element_type=jnp.float32
        )
        * scale
    )
    wide_key_grad = (
        jnp.einsum(
            "shgqk,shgqd->shkd", wide_scores_grad, global_query, preferred_element_type=jnp.float32
        )
        * scale
    )
    wide_value_grad = jnp.einsum(
        "shgqk,shgqd->shkd", wide_probs_low, wide_grad, preferred_element_type=jnp.float32
    )
    wide_pair_grad = jnp.concatenate([wide_key_grad, wide_value_grad], axis=-1).reshape(
        seqs, heads, per_dev, BLK, pair_width
    )
    rim_pair = jnp.concatenate([window_grads[:, :, 0], window_grads[:, :, per_dev + 1]], axis=2)
    rim_back = extended(rim_pair.astype(jnp.bfloat16), (("ctx", 2),), BLK).astype(rim_pair.dtype)
    local_grad = window_grads[:, :, 1 : per_dev + 1] + wide_pair_grad
    local_grad = local_grad.at[:, :, 0].add(rim_back[:, :, :BLK])
    local_grad = local_grad.at[:, :, per_dev - 1].add(rim_back[:, :, 3 * BLK :])
    global_total, wide_query = lax.psum((global_grads, wide_query_part), "ctx")
    local_grad = local_grad.at[:, :, 0].add(jnp.where(first_owner, global_total[:, :, 0], 0.0))
    local_grad = local_grad.at[:, :, per_dev - 1].add(
        jnp.where(last_owner, global_total[:, :, 1], 0.0)
    )
    query_grads = query_grads.at[:, :, :BLK].add(jnp.where(first_owner, wide_query[:, :, 0], 0.0))
    query_grads = query_grads.at[:, :, length - BLK :].add(
        jnp.where(last_owner, wide_query[:, :, 1], 0.0)
    )
    local_grad = local_grad + random_total.reshape(seqs, heads, per_dev, BLK, pair_width)
    pair_grad = local_grad.reshape(seqs, heads, length, pair_width).transpose(2, 0, 1, 3)
    query_part = query_grads.transpose(2, 0, 1, 3)
    projected_grad = jnp.concatenate([query_part, pair_grad], axis=-1).astype(jnp.bfloat16)
    projected_rows = projected_grad.reshape(total_rows, heads * 3 * head_dim)
    grad_in = (
        (residual_grad + rows_sum(projected_rows, input_low, 1))
        .astype(jnp.bfloat16)
        .reshape(part_rows, seqs, width)
    )
    input_grad = outer_sum(x_rows, projected_rows).reshape(width, heads, 3 * head_dim)
    pair_bias_grad = jnp.stack(
        [
            jnp.sum(projected_grad[..., :head_dim], axis=(0, 1), dtype=jnp.float32).reshape(-1),
            jnp.sum(projected_grad[..., 2 * head_dim :], axis=(0, 1), dtype=jnp.float32).reshape(
                -1
            ),
        ]
    )
    output_grad = outer_sum(mixed, branch_full)
    bias_grad = jnp.stack(
        [
            jnp.sum(branch_low, axis=0, dtype=jnp.float32),
            jnp.sum(second_low, axis=0, dtype=jnp.float32),
        ]
    )
    gain_grad = jnp.stack(
        [jnp.sum(first_grad * normed_one, axis=0), jnp.sum(upstream * normed_two, axis=0)]
    )
    shift_grad = jnp.stack([jnp.sum(first_grad, axis=0), jnp.sum(upstream, axis=0)])
    upper_grad = outer_sum(first_full, inner_low)
    upper_bias_grad = jnp.sum(inner_low, axis=0, dtype=jnp.float32)
    lower_grad = outer_sum(active, second_full)
    shares = (
        lax.psum_scatter(input_grad, "fsdp", scatter_dimension=0, tiled=True),
        lax.psum_scatter(pair_bias_grad, "fsdp", scatter_dimension=1, tiled=True),
        lax.psum_scatter(output_grad, "fsdp", scatter_dimension=1, tiled=True),
        lax.psum_scatter(bias_grad, "fsdp", scatter_dimension=1, tiled=True),
        lax.psum_scatter(gain_grad, "fsdp", scatter_dimension=1, tiled=True),
        lax.psum_scatter(shift_grad, "fsdp", scatter_dimension=1, tiled=True),
        lax.psum_scatter(upper_grad, "fsdp", scatter_dimension=0, tiled=True),
        lax.psum_scatter(upper_bias_grad, "fsdp", scatter_dimension=0, tiled=True),
        lax.psum_scatter(lower_grad, "fsdp", scatter_dimension=1, tiled=True),
    )
    matrices = lax.psum((shares[0], shares[1], shares[2], shares[6], shares[7], shares[8]), "ctx")
    vectors = lax.psum((shares[3], shares[4], shares[5]), ("ctx", "tp"))
    return (
        layer_out,
        grad_in,
        matrices[0],
        matrices[1],
        matrices[2],
        vectors[0],
        vectors[1],
        vectors[2],
        matrices[3],
        matrices[4],
        matrices[5],
    )


def solution(mesh):
    placed = (
        P(("ctx", "tp"), "fsdp", None),
        P("fsdp", None, "tp", None),
        P("fsdp", "tp", None),
        P(None, ("tp", "fsdp")),
        P("tp", "fsdp"),
        P(None, "fsdp"),
        P(None, "fsdp"),
        P(None, "fsdp"),
        P("fsdp", "tp"),
        P(("tp", "fsdp")),
        P("tp", "fsdp"),
        P(("ctx", "tp"), "fsdp", None),
    )
    return jax.shard_map(
        shards,
        mesh=mesh,
        in_specs=placed,
        out_specs=(
            P(("ctx", "tp"), "fsdp", None),
            P(("ctx", "tp"), "fsdp", None),
            P("fsdp", "tp", None),
            P(None, ("tp", "fsdp")),
            P("tp", "fsdp"),
            P(None, "fsdp"),
            P(None, "fsdp"),
            P(None, "fsdp"),
            P("fsdp", "tp"),
            P(("tp", "fsdp")),
            P("tp", "fsdp"),
        ),
        check_vma=False,
    )
```

profile of v0, /device:TPU:11, one launch (start us, length us, event | category | flops | bytes accessed | tf_op | source)
XLA Modules:
  0.0 1863.9 jit_solution(15493732854384681675)
XLA Ops:
  41.1 31.4 %all-gather.21.cloned.1.call-done = bf16[512,4,768]{2,0,1:T(8,128)(2,1)} async-done(((bf16[128,4,768]{2,0,1:T(8,128)(2,1)}), bf16[512,4,768]{2,0,1:T(8,128)(2,1)}) %all-gather.21.cloned.1.call-update) | async-done | bytes 3145744 | tf_op jit(solution)/shard_map/all_gather | solution.py:70
  106.5 18.7 %all-reduce.24.cloned.1.call-done = (bf16[4,3,1,64,192]{4,3,2,1,0:T(8,128)(2,1)}, bf16[4,3,1,64,192]{4,3,2,1,0:T(8,128)(2,1)}) async-done(((bf16[4,3,1,64,192]{4,3,2,1,0:T(8,128)(2,1)}, bf16[4,3,1,64,192]{4,3,2,1,0:T(8,128)(2,1)}), (bf16[4,3,1,64,192]{4,3,2,1,0:T(8,128)(2,1)}, bf16[4,3,1,64,192]{4,3,2,1,0:T(8,128)(2,1)})) %all-reduce.24.cloned.1.call-update) | async-done | bytes 589840 | tf_op jit(solution)/shard_map/psum | solution.py:15
  131.2 94.3 %while.52 = (s32[]{:T(128)}, bf16[4,1,3,8,64,64]{5,4,3,2,1,0:T(8,128)(2,1)}, f32[4,1,3,8,64]{4,3,2,1,0:T(8,128)}, bf16[4,1,3,8,64,64]{5,4,3,2,1,0:T(8,128)(2,1)}...) while((s32[]{:T(128)}, ...), condition=%wide.region_5.6_spmd.clone, body=%wide.region_2.5_spmd.clone.sunk | while | flops 210861760 | bytes 34393680 | solution.py:314
  235.9 19.6 %all-reduce.25 = bf16[4,3,2,64,64]{4,3,2,1,0:T(8,128)(2,1)S(1)} all-reduce(f32[4,3,2,64,64]{4,3,2,1,0:T(8,128)S(1)} %fusion.84), channel_id=1, replica_groups=mesh['fsdp'=4,'ctx'=2,'tp'=4] {'ctx'}, use_global_device_ids=true, to_apply=%region_8.9 | all-reduce | flops 98304 | bytes 589824 | tf_op jit(solution)/shard_map/psum | solution.py:279
  291.7 93.4 %reduce-scatter.29.cloned.1.call-done = f32[512,768]{1,0:T(8,128)} async-done(((f32[2048,768]{1,0:T(8,128)}), f32[512,768]{1,0:T(8,128)}) %reduce-scatter.29.cloned.1.call-update) | async-done | bytes 1572880 | tf_op jit(solution)/shard_map/reduce_scatter | solution.py:74
  398.6 51.8 %all-gather.23.cloned.1.call-done = bf16[512,4,768]{2,1,0:T(4,128)(2,1)} async-done(((bf16[128,4,768]{2,1,0:T(4,128)(2,1)}), bf16[512,4,768]{2,1,0:T(4,128)(2,1)}) %all-gather.23.cloned.1.call-update) | async-done | bytes 3145744 | tf_op jit(solution)/shard_map/all_gather | solution.py:70
  456.4 15.0 all-gather.25.cloned.1.call-done
  471.4 19.0 %multiply_convert_fusion.1 = (bf16[2048,768]{1,0:T(8,128)(2,1)}, f32[2048,768]{1,0:T(8,128)}, f32[2048,768]{1,0:T(8,128)}) fusion(f32[768]{0:T(1024)S(1)} %convert_element_type.202, bf16[2048,768]{1,0:T(8,128)(2,1)} %reshape.1106, bf16[768,768]{1,0:T(8,128)(2,1)} %all-gather.25.cloned.1.call-done), kind=kOutput, calls=%fused_computation.117 | convolution fusion | flops 2519728128 | bytes 20057088 | tf_op jit(solution)/shard_map/dot_general | solution.py:336
  505.0 104.0 %reduce-scatter.31.cloned.1.call-done = f32[512,768]{1,0:T(8,128)} async-done(((f32[2048,768]{1,0:T(8,128)}), f32[512,768]{1,0:T(8,128)}) %reduce-scatter.31.cloned.1.call-update) | async-done | bytes 1572880 | tf_op jit(solution)/shard_map/reduce_scatter | solution.py:74
  617.8 61.7 %all-gather.29.cloned.1.call-done = bf16[512,4,768]{2,1,0:T(4,128)(2,1)} async-done(((bf16[128,4,768]{2,1,0:T(4,128)(2,1)}), bf16[512,4,768]{2,1,0:T(4,128)(2,1)}) %all-gather.29.cloned.1.call-update) | async-done | bytes 3145744 | tf_op jit(solution)/shard_map/all_gather | solution.py:70
  702.9 111.9 %reduce-scatter.33.cloned.1.call-done = f32[512,768]{1,0:T(8,128)} async-done(((f32[2048,768]{1,0:T(8,128)}), f32[512,768]{1,0:T(8,128)}) %reduce-scatter.33.cloned.1.call-update) | async-done | bytes 1572880 | tf_op jit(solution)/shard_map/reduce_scatter | solution.py:74
  821.3 61.5 %all-gather.31.cloned.1.call-done = bf16[512,4,768]{2,1,0:T(4,128)(2,1)} async-done(((bf16[128,4,768]{2,1,0:T(4,128)(2,1)}), bf16[512,4,768]{2,1,0:T(4,128)(2,1)}) %all-gather.31.cloned.1.call-update) | async-done | bytes 3145744 | tf_op jit(solution)/shard_map/all_gather | solution.py:70
  910.3 17.7 all-reduce.22.cloned.1.call-done
  929.9 35.2 %all-reduce.16.cloned.1.call-done = f32[4,3,2,64,64]{4,3,1,0,2:T(8,128)} async-done(((f32[4,3,2,64,64]{4,3,1,0,2:T(8,128)}), f32[4,3,2,64,64]{4,3,1,0,2:T(8,128)}) %all-reduce.16.cloned.1.call-update) | async-done | bytes 393232 | tf_op jit(solution)/shard_map/psum | solution.py:279
  970.3 418.0 %while.53 = (s32[]{:T(128)}, f32[4,1,3,8,64,64]{5,4,3,2,1,0:T(8,128)}, f32[4,1,3,10,64,128]{5,4,2,0,3,1:T(8,128)}, f32[4,1,3,2,64,128]{5,4,3,2,0,1:T(8,128)}, f3...) while((s32[]{:T(128)}, ...), condition=%wide.region_25.26_spmd.clone, body=%wide.region_20.25_spmd.clone.sunk | while | flops 513196576 | bytes 199906496 | solution.py:413
  1494.3 14.5 reduce-scatter.39.cloned.1.call-done
  1508.8 35.5 %reduce-scatter.41.cloned.1.call-done = f32[768,192]{0,1:T(8,128)} async-done(((f32[768,768]{0,1:T(8,128)}), f32[768,192]{0,1:T(8,128)}) %reduce-scatter.41.cloned.1.call-update) | async-done | bytes 589840 | tf_op jit(solution)/shard_map/reduce_scatter | solution.py:508
  1544.3 35.8 %reduce-scatter.37.cloned.1.call-done = f32[192,3,192]{2,0,1:T(8,128)} async-done(((f32[768,3,192]{2,0,1:T(8,128)}), f32[192,3,192]{2,0,1:T(8,128)}) %reduce-scatter.37.cloned.1.call-update) | async-done | bytes 442384 | tf_op jit(solution)/shard_map/reduce_scatter | solution.py:500
  1587.7 16.4 reduce-scatter.51.cloned.1.call-done
  1605.1 23.0 %reduce-scatter.47.cloned.1.call-done = f32[192,2]{1,0:T(8,128)} async-done(((f32[768,2]{1,0:T(8,128)}), f32[192,2]{1,0:T(8,128)}) %reduce-scatter.47.cloned.1.call-update) | async-done | bytes 1552
  1629.0 22.8 %reduce-scatter.49.cloned.1.call-done = f32[192,2]{1,0:T(8,128)} async-done(((f32[768,2]{1,0:T(8,128)}), f32[192,2]{1,0:T(8,128)}) %reduce-scatter.49.cloned.1.call-update) | async-done | bytes 1552
  1652.8 15.0 all-reduce.3
  1679.1 108.3 %reduce-scatter.35.cloned.1.call-done = f32[512,768]{1,0:T(8,128)} async-done(((f32[2048,768]{1,0:T(8,128)}), f32[512,768]{1,0:T(8,128)}) %reduce-scatter.35.cloned.1.call-update) | async-done | bytes 1572880 | tf_op jit(solution)/shard_map/reduce_scatter | solution.py:74
  1790.0 60.5 %all-reduce.18.cloned.1.call-done = (f32[192,3,192]{2,0,1:T(8,128)}, f32[192,192]{1,0:T(8,128)}, f32[192,768]{1,0:T(8,128)}, f32[768,192]{0,1:T(8,128)}) async-done(((f32[192,3,192]{2,0,1:T(8,128)}, f32[192,192]{1,0:T(8,128)}, f32[192,768]{1,0:T(8,128)}, f32[768,192]{0,1:T(8,128)}), (f32[192,3,192]{2,0,1:T(8,128)}, f32[192,192]{1,0:T(8,128)}, f32[192,768]{1,0:T(8,128)}, ...) | async-done | bytes 1769488 | tf_op jit(solution)/shard_map/psum | solution.py:510
  (694 shorter events, 872.6 us)
Async XLA Ops:
  9.4 115.8 %all-reduce.24.cloned.1.call-start = ((), (), s32[]{:S(2)}) async-start(), calls=%async_computation.35 | async-start | bytes 1572864 | tf_op jit(solution)/shard_map/psum | solution.py:15
  82.7 302.5 %reduce-scatter.29.cloned.1.call-start = ((), (), s32[]{:S(2)}) async-start(), calls=%async_computation.14 | async-start | bytes 7864320 | tf_op jit(solution)/shard_map/reduce_scatter | solution.py:74
  266.8 183.6 %all-gather.23.cloned.1.call-start = ((), (), s32[]{:S(2)}) async-start(), calls=%async_computation.15 | async-start | bytes 3932160 | tf_op jit(solution)/shard_map/all_gather | solution.py:70
  388.6 82.7 %all-gather.25.cloned.1.call-start = ((), (), s32[]{:S(2)}) async-start(), calls=%async_computation.16 | async-start | bytes 1474560 | tf_op jit(solution)/shard_map/all_gather | solution.py:222
  389.5 101.5 %all-gather.27.cloned.1.call-start = ((), (), s32[]{:S(2)}) async-start(), calls=%async_computation.17 | async-start | bytes 1474560 | tf_op jit(solution)/shard_map/all_gather | solution.py:224
  391.4 217.6 %reduce-scatter.31.cloned.1.call-start = ((), (), s32[]{:S(2)}) async-start(), calls=%async_computation.18 | async-start | bytes 7864320 | tf_op jit(solution)/shard_map/reduce_scatter | solution.py:74
  498.4 181.1 %all-gather.29.cloned.1.call-start = ((), (), s32[]{:S(2)}) async-start(), calls=%async_computation.19 | async-start | bytes 3932160 | tf_op jit(solution)/shard_map/all_gather | solution.py:70
  617.8 197.0 %reduce-scatter.33.cloned.1.call-start = ((), (), s32[]{:S(2)}) async-start(), calls=%async_computation.20 | async-start | bytes 7864320 | tf_op jit(solution)/shard_map/reduce_scatter | solution.py:74
  702.8 179.9 %all-gather.31.cloned.1.call-start = ((), (), s32[]{:S(2)}) async-start(), calls=%async_computation.21 | async-start | bytes 3932160 | tf_op jit(solution)/shard_map/all_gather | solution.py:70
  821.0 107.0 %all-reduce.22.cloned.1.call-start = ((), (), s32[]{:S(2)}) async-start(), calls=%async_computation.34 | async-start | bytes 786432 | tf_op jit(solution)/shard_map/psum | solution.py:368
  970.3 103.4 %reduce-scatter.53.cloned.1.call-start = ((), (), s32[]{:S(2)}) async-start(), calls=%async_computation.36 | async-start | bytes 1179648 | tf_op jit(solution)/shard_map/while
  1075.7 102.4 %reduce-scatter.53.cloned.1.call-start = ((), (), s32[]{:S(2)}) async-start(), calls=%async_computation.36 | async-start | bytes 1179648 | tf_op jit(solution)/shard_map/while
  1180.1 101.8 %reduce-scatter.53.cloned.1.call-start = ((), (), s32[]{:S(2)}) async-start(), calls=%async_computation.36 | async-start | bytes 1179648 | tf_op jit(solution)/shard_map/while
  1284.0 101.9 %reduce-scatter.53.cloned.1.call-start = ((), (), s32[]{:S(2)}) async-start(), calls=%async_computation.36 | async-start | bytes 1179648 | tf_op jit(solution)/shard_map/while
  1388.9 103.6 %reduce-scatter.45.cloned.1.call-start = ((), (), s32[]{:S(2)}) async-start(), calls=%async_computation.28 | async-start | bytes 983040
  1393.6 115.3 %reduce-scatter.39.cloned.1.call-start = ((), (), s32[]{:S(2)}) async-start(), calls=%async_computation.25 | async-start | bytes 2949120 | tf_op jit(solution)/shard_map/reduce_scatter | solution.py:506
  1399.6 144.7 %reduce-scatter.41.cloned.1.call-start = ((), (), s32[]{:S(2)}) async-start(), calls=%async_computation.26 | async-start | bytes 2949120 | tf_op jit(solution)/shard_map/reduce_scatter | solution.py:508
  1413.8 166.4 %reduce-scatter.37.cloned.1.call-start = ((), (), s32[]{:S(2)}) async-start(), calls=%async_computation.24 | async-start | bytes 2949120 | tf_op jit(solution)/shard_map/reduce_scatter | solution.py:500
  1478.7 125.4 %reduce-scatter.51.cloned.1.call-start = ((), (), s32[]{:S(2)}) async-start(), calls=%async_computation.31 | async-start | bytes 491520
  1479.8 148.2 %reduce-scatter.47.cloned.1.call-start = ((), (), s32[]{:S(2)}) async-start(), calls=%async_computation.29 | async-start | bytes 491520
  1480.9 171.0 %reduce-scatter.49.cloned.1.call-start = ((), (), s32[]{:S(2)}) async-start(), calls=%async_computation.30 | async-start | bytes 491520
  1481.9 192.0 %reduce-scatter.43.cloned.1.call-start = ((), (), s32[]{:S(2)}) async-start(), calls=%async_computation.27 | async-start | bytes 122880
  1485.2 302.2 %reduce-scatter.35.cloned.1.call-start = ((), (), s32[]{:S(2)}) async-start(), calls=%async_computation.23 | async-start | bytes 7864320 | tf_op jit(solution)/shard_map/reduce_scatter | solution.py:74
  1492.4 358.1 %all-reduce.18.cloned.1.call-start = ((), (), s32[]{:S(2)}) async-start(), calls=%async_computation.32 | async-start | bytes 3932160 | tf_op jit(solution)/shard_map/psum | solution.py:510
  (83 other events, 1647.4 us)
Sparse Core Ops, SparseCore 0:
  10.2 62.2 all-gather.20
  82.8 42.4 all-reduce.23
  266.9 118.2 reduce-scatter.28
  388.8 61.5 all-gather.22
  498.6 110.3 reduce-scatter.30
  617.9 61.5 all-gather.28
  703.0 111.8 reduce-scatter.32
  821.2 61.5 all-gather.30
  902.0 25.9 all-reduce.21
  930.7 34.3 all-reduce.15
  1158.4 19.0 reduce-scatter.52
  1261.9 20.0 reduce-scatter.52
  1365.3 20.5 reduce-scatter.52
  1391.9 53.8 all-reduce.19
  1448.2 24.8 reduce-scatter.44
  1475.7 33.0 reduce-scatter.38
  1511.2 33.0 reduce-scatter.40
  1547.0 33.0 reduce-scatter.36
  1583.2 20.8 reduce-scatter.50
  1607.2 20.8 reduce-scatter.46
  1631.0 20.8 reduce-scatter.48
  1654.8 19.0 reduce-scatter.42
  1676.1 111.2 reduce-scatter.34
  1790.3 60.1 all-reduce.17
  (3 shorter events, 54.5 us)
where the time goes:
time: 1880 us; the launch traced here: 1860 us
  waiting for transfers between devices  955 us (51%)
  local copies, waits for them, and re-layouts  360 us (19%)
  blocking collectives  180 us (10%)
  matrix products  172 us (9%)
  other arithmetic  164 us (9%)
    reduce_scatter x4, waiting for transfers between devices, rows_sum(): lax.psum_scatter(lax.dot_general(left, right, (((1,), (contract,)), ((),...  418 us
    all_gather x4, waiting for transfers between devices, rows_all(): return lax.all_gather(value, 'tp', axis=0, tiled=True)  206 us
    all_gather x8, blocking collectives, random_pairs_for(): whole = lax.all_gather(block_group, 'ctx', axis=2, tiled=True)  75 us
    while x100, local copies, waits for them, and re-layouts  69.4 us
    unnamed x28, waiting for transfers between devices  69.3 us
    psum x1, waiting for transfers between devices, shards(): lax.psum((shares[0], shares[1], shares[2], shares[6], shares[7], shares[8...  60.5 us
    scatter-add x4, other arithmetic, random_back(): spread_grad = jnp.zeros((group, heads, blocks_all, BLK, pair_width), jnp....  53.1 us
    concatenate x12, local copies, waits for them, and re-layouts, attend_back(): pairs_grad = jnp.concatenate([keys_grad, values_grad], axis=-1)  48.8 us
  transfers between devices with their start and end apart: 31, of which 26 were waited for; matrix products, arithmetic and copies ran while one was open for 12% of the time, Pallas kernels for 0%

commit v1 on v0

--- a/solution.py
+++ b/solution.py
@@ -1,6 +1,8 @@
 import jax
 import jax.numpy as jnp
 from jax import lax
+from jax.experimental import pallas as pl
+from jax.experimental.pallas import tpu as pltpu
 from jax.sharding import PartitionSpec as P
 
 BLK = 64
@@ -181,7 +183,7 @@
     return (query_grad, window_grad, global_grad, random_grad)
 
 
-def shards(
+def span_shards(
     hidden_in,
     rand_blocks,
     w_in,
@@ -283,8 +285,6 @@
     table = table.transpose(0, 1, 2, 4, 3).reshape(units, ctx_count)
     mine = lax.dynamic_index_in_dim(table, ctx_place, 1, keepdims=False)
     mine_groups = mine.reshape(steps, group, heads, picks, per_dev)
-    seq_pick = jnp.arange(group)[:, None, None, None]
-    head_pick = jnp.arange(heads)[None, :, None, None]
     block_index = ctx_place * per_dev + jnp.arange(per_dev)
     present = jnp.concatenate(
         [
@@ -299,7 +299,10 @@
 
     def random_pairs_for(block_group, id_group):
         whole = lax.all_gather(block_group, "ctx", axis=2, tiled=True)
-        return whole[seq_pick, head_pick, id_group]
+        chosen = jax.nn.one_hot(id_group, blocks_all, dtype=jnp.bfloat16)
+        return jnp.einsum(
+            "shpqb,shbke->shpqke", chosen, whole, preferred_element_type=jnp.float32
+        ).astype(jnp.bfloat16)
 
     query_groups = split_groups(query_heads, steps, group)
     pad_groups = split_groups(window_pad, steps, group)
@@ -377,10 +380,9 @@
     )
 
     def random_back(random_grad, id_group):
-        spread_grad = (
-            jnp.zeros((group, heads, blocks_all, BLK, pair_width), jnp.float32)
-            .at[seq_pick, head_pick, id_group]
-            .add(random_grad)
+        chosen = jax.nn.one_hot(id_group, blocks_all, dtype=jnp.float32)
+        spread_grad = jnp.einsum(
+            "shpqb,shpqke->shbke", chosen, random_grad, precision=lax.Precision.HIGHEST
         )
         return lax.psum_scatter(
             spread_grad.astype(jnp.bfloat16), "ctx", scatter_dimension=2, tiled=True
@@ -524,6 +526,1060 @@
     )
 
 
+MESH = pl.DeviceIdType.MESH
+BF = jnp.bfloat16
+F32 = jnp.float32
+NT = (((1,), (1,)), ((), ()))
+NN = (((1,), (0,)), ((), ()))
+TN = (((0,), (0,)), ((), ()))
+VMEM_LIMIT = 58 * 2**20
+
+
+def mm(left, right, dims=NN):
+    return lax.dot_general(left, right, dims, preferred_element_type=F32)
+
+
+class Place:
+    def __init__(self):
+        self.f = lax.axis_index("fsdp")
+        self.c = lax.axis_index("ctx")
+        self.t = lax.axis_index("tp")
+        f, c, t = self.f, self.c, self.t
+        self.k = k = lax.rem(f, 2)
+        self.y = y = f // 2
+        self.p = t + k * (3 - 2 * t)
+        self.core = (f + 1 - 2 * k, c, t)
+        self.xnbr = (f, 1 - c, t)
+        self.ynbr = (lax.rem(f + 2, 4), c, t)
+        self.zplus = (f, c, t + 1 - 2 * k)
+        self.zminus = (f, c, t - 1 + 2 * k)
+        self.own_core = t // 2
+        self.own_slot = t + (t // 2) * (3 - 2 * t)
+        self.pair = 2 * y
+        self.other = 2 - 2 * y
+
+    def swap(self, s):
+        return (2 * self.y + self.c, self.k, s)
+
+    def swap_is_self(self, s):
+        return jnp.logical_and(self.k == self.c, self.t == s)
+
+
+def copy_to(src, dst, send, recv, device):
+    return pltpu.make_async_remote_copy(
+        src_ref=src, dst_ref=dst, send_sem=send, recv_sem=recv, device_id=device, device_id_type=MESH
+    )
+
+
+def greet(at):
+    barrier = pltpu.get_barrier_semaphore()
+    sizes = [lax.axis_size(a) for a in ("fsdp", "ctx", "tp")]
+    others = 0
+    for i in range(sizes[0]):
+        for j in range(sizes[1]):
+            for m in range(sizes[2]):
+                if i or j or m:
+                    others += 1
+                    device = (
+                        lax.rem(at.f + i, sizes[0]),
+                        lax.rem(at.c + j, sizes[1]),
+                        lax.rem(at.t + m, sizes[2]),
+                    )
+                    pl.semaphore_signal(barrier, inc=1, device_id=device, device_id_type=MESH)
+    pl.semaphore_wait(barrier, others)
+
+
+class Gather:
+    def __init__(self, at, shards, full, send, recv):
+        self.at, self.shards, self.full, self.send, self.recv = at, shards, full, send, recv
+
+    def own(self, g):
+        at, full, shard = self.at, self.full[g], self.shards[g]
+        half = shard.shape[0] // 2
+        rows = pl.ds(pl.multiple_of(at.c * half, half), half)
+
+        @pl.when(at.k == at.own_core)
+        def _():
+            full[at.own_slot, at.f, at.c] = shard[rows, :]
+
+        @pl.when(at.k != at.own_core)
+        def _():
+            self.cp(g, at.own_slot, 0, shard.at[rows], full.at[at.own_slot, at.f, at.c], at.core).start()
+
+    def cp(self, g, slot, kind, src, dst, device):
+        return copy_to(src, dst, self.send.at[g, slot, kind], self.recv.at[g, slot, kind], device)
+
+    def arrives(self, g, slot, kind, dst):
+        self.cp(g, slot, kind, dst, dst, self.at.core).wait_recv()
+
+    def ours(self, g, slot, f, c):
+        return self.full[g].at[slot, pl.ds(f, 2), c]
+
+    def step_z(self, g, turn):
+        at, full = self.at, self.full[g]
+        first = (at.p + 2) // 3
+        slot = first if turn == 0 else 1 - first
+        piece = self.ours(g, slot, at.pair, at.c)
+
+        @pl.when(at.p == slot)
+        def _():
+            self.arrives(g, slot, 0, full.at[slot, at.core[0], at.c])
+
+        @pl.when(at.p > slot)
+        def _():
+            self.arrives(g, slot, 1, piece)
+
+        @pl.when(at.p < slot)
+        def _():
+            self.arrives(g, slot, 2, piece)
+
+        @pl.when(jnp.logical_and(at.p >= slot, at.p < 3))
+        def _():
+            self.cp(g, slot, 1, piece, piece, at.zplus).start()
+
+        @pl.when(jnp.logical_and(at.p == 1, slot == 1))
+        def _():
+            self.cp(g, slot, 2, piece, piece, at.zminus).start()
+
+        self.cp(g, slot, 3, piece, piece, at.ynbr).start()
+        self.cp(g, slot, 4, piece, piece, at.xnbr).start()
+
+    def step_relay(self, g, turn):
+        at, full = self.at, self.full[g]
+        first = (at.p + 2) // 3
+        slot = first if turn == 0 else 1 - first
+        self.arrives(g, slot, 3, self.ours(g, slot, at.other, at.c))
+        even = full.at[slot, at.other, at.c]
+        self.cp(g, slot, 5, even, even, at.xnbr).start()
+        self.arrives(g, slot, 4, self.ours(g, slot, at.pair, 1 - at.c))
+        odd = full.at[slot, at.pair + 1, 1 - at.c]
+        self.cp(g, slot, 6, odd, odd, at.ynbr).start()
+
+    def step_last(self, g):
+        at, full = self.at, self.full[g]
+        for slot in range(2):
+            self.arrives(g, slot, 5, full.at[slot, at.other, 1 - at.c])
+            self.arrives(g, slot, 6, full.at[slot, at.other + 1, 1 - at.c])
+
+    def sent(self, g):
+        at, full = self.at, self.full[g]
+
+        def left(slot, kind, src):
+            self.cp(g, slot, kind, src, src, at.core).wait_send()
+
+        @pl.when(at.k != at.own_core)
+        def _():
+            left(at.own_slot, 0, full.at[at.own_slot, at.f, at.c])
+
+        for slot in range(2):
+            piece = self.ours(g, slot, at.pair, at.c)
+
+            @pl.when(jnp.logical_and(at.p >= slot, at.p < 3))
+            def _():
+                left(slot, 1, piece)
+
+            if slot == 1:
+
+                @pl.when(at.p == 1)
+                def _():
+                    left(slot, 2, piece)
+
+            left(slot, 3, piece)
+            left(slot, 4, piece)
+            left(slot, 5, full.at[slot, at.other, at.c])
+            left(slot, 6, full.at[slot, at.pair + 1, 1 - at.c])
+
+
+class Swap:
+    def __init__(self, at, blocks, rows, base, send, recv):
+        self.at, self.blocks, self.rows, self.base, self.send, self.recv = at, blocks, rows, base, send, recv
+        self.n = blocks.shape[1]
+
+    def span(self, s, base):
+        return pl.ds(pl.multiple_of(base + s * self.n, self.n), self.n)
+
+    def start_in(self):
+        at = self.at
+        there = self.rows.at[self.span(at.t, self.base * at.c)]
+        for s in range(4):
+
+            @pl.when(at.swap_is_self(s))
+            def _():
+                self.rows[self.span(s, self.base * at.k), :] = self.blocks[s]
+
+            @pl.when(jnp.logical_not(at.swap_is_self(s)))
+            def _():
+                copy_to(self.blocks.at[s], there, self.send.at[s], self.recv.at[at.t], at.swap(s)).start()
+
+    def wait_in(self, s):
+        at = self.at
+        here = self.rows.at[self.span(s, self.base * at.k)]
+
+        @pl.when(jnp.logical_not(at.swap_is_self(s)))
+        def _():
+            copy_to(here, here, self.send.at[s], self.recv.at[s], at.core).wait_recv()
+
+    def start_out(self, s):
+        at = self.at
+        here = self.rows.at[self.span(s, self.base * at.k)]
+
+        @pl.when(at.swap_is_self(s))
+        def _():
+            self.blocks[s] = self.rows[self.span(s, self.base * at.k), :]
+
+        @pl.when(jnp.logical_not(at.swap_is_self(s)))
+        def _():
+            copy_to(here, self.blocks.at[at.t], self.send.at[s], self.recv.at[at.t], at.swap(s)).start()
+
+    def wait_out(self, s):
+        at = self.at
+
+        @pl.when(jnp.logical_not(at.swap_is_self(s)))
+        def _():
+            copy_to(self.blocks.at[s], self.blocks.at[s], self.send.at[s], self.recv.at[s], at.core).wait_recv()
+
+    def sent(self):
+        at = self.at
+        for s in range(4):
+
+            @pl.when(jnp.logical_not(at.swap_is_self(s)))
+            def _():
+                copy_to(self.blocks.at[s], self.blocks.at[s], self.send.at[s], self.recv.at[s], at.core).wait_send()
+QCHUNK = 256
+
+
+def attend_chunk(h, q, key, query, value_t, bias, lse, mixed_t, spots):
+    cols = pl.ds(pl.multiple_of(q * QCHUNK, QCHUNK), QCHUNK)
+    scores = mm(key[h], query[h, cols, :], NT)
+    length = scores.shape[0]
+    scores = (
+        scores.reshape(length // BLK, BLK, QCHUNK) + bias[h, :, cols][:, None, :]
+    ).reshape(length, QCHUNK)
+    top = jnp.max(scores, axis=0, keepdims=True)
+    weights = jnp.exp(scores - top)
+    total = jnp.sum(weights, axis=0, keepdims=True)
+    probs = (weights * (1.0 / total)).astype(BF)
+    lse[h, :, cols] = top + jnp.log(total)
+    mixed_t[spots(h), cols] = mm(value_t[h], probs)
+
+
+def forward_kernel(
+    xs, cs, shard0, shard1, shard2, bias, proj_bias, proj_scale,
+    x_all, up_half, full0, full1, full2, query, key, value, mixed, lse,
+    value_t, mixed_t,
+    xs_send, xs_recv, xc_send, xc_recv, cs_send, cs_recv, w_send, w_recv,
+):
+    at = Place()
+    greet(at)
+    gather = Gather(at, (shard0, shard1, shard2), (full0, full1, full2), w_send, w_recv)
+    tokens = Swap(at, xs, x_all, 512, xs_send, xs_recv)
+    grads = Swap(at, cs, up_half, 0, cs_send, cs_recv)
+    part = xs.shape[1]
+    tokens.start_in()
+    for g in range(3):
+        gather.own(g)
+    gather.step_z(0, 0)
+    gather.step_z(0, 1)
+    gather.step_relay(0, 0)
+    gather.step_relay(0, 1)
+
+    def to_core(s, half):
+        rows = x_all.at[pl.ds(pl.multiple_of(half * 512 + s * part, part), part)]
+        return copy_to(rows, rows, xc_send.at[s], xc_recv.at[s], at.core)
+
+    for s in range(4):
+        tokens.wait_in(s)
+        to_core(s, at.k).start()
+    gather.step_z(1, 0)
+    gather.step_z(1, 1)
+    grads.start_in()
+    for s in range(4):
+        to_core(s, 1 - at.k).wait_recv()
+    gather.step_last(0)
+
+    heads = query.shape[0]
+    dim = query.shape[2]
+    width = x_all.shape[1]
+    for slot in range(2):
+
+        @pl.loop(0, 4)
+        def _(r):
+            rows = pl.ds(pl.multiple_of(r * 256, 256), 256)
+            weight = full0[slot, :, :, :, 0:640].reshape(width, 640)
+            got = (mm(x_all[rows, :], weight) + proj_bias[slot]) * proj_scale[...]
+            for i in range(heads // 2):
+                h = slot * (heads // 2) + i
+                start = i * 3 * dim
+                query[h, rows, :] = got[:, start : start + dim].astype(BF)
+                key[h, rows, :] = got[:, start + dim : start + 2 * dim].astype(BF)
+                one = got[:, start + 2 * dim : start + 3 * dim]
+                value[h, rows, :] = one.astype(BF)
+                value_t[h, :, rows] = one.T.astype(BF)
+
+    gather.step_relay(1, 0)
+    gather.step_relay(1, 1)
+    gather.step_z(2, 0)
+    gather.step_z(2, 1)
+    for slot in range(2):
+        mixed_t[slot * 256 : slot * 256 + dim, :] = jnp.zeros((dim, mixed_t.shape[1]), F32)
+
+    def spots(h):
+        return pl.ds(pl.multiple_of((h // 3) * 256 + (h % 3 + 1) * dim, dim), dim)
+
+    def attend(low_head, high_head):
+        @pl.loop(low_head, high_head)
+        def _(h):
+            @pl.loop(0, 1024 // QCHUNK)
+            def _(q):
+                attend_chunk(h, q, key, query, value_t, bias, lse, mixed_t, spots)
+
+    attend(0, 2)
+    gather.step_relay(2, 0)
+    gather.step_relay(2, 1)
+    gather.step_last(1)
+    attend(2, 6)
+
+    @pl.loop(0, 4)
+    def _(r):
+        rows = pl.ds(pl.multiple_of(r * 256, 256), 256)
+        mixed[rows, :] = mixed_t[:, rows].T.astype(BF)
+
+    gather.step_last(2)
+    for s in range(4):
+        grads.wait_in(s)
+        to_core(s, at.k).wait_send()
+    tokens.sent()
+    grads.sent()
+    for g in range(3):
+        gather.sent(g)
+
+
+def vmem():
+    return pl.BlockSpec(memory_space=pltpu.VMEM)
+
+
+def forward_call(xs, cs, shards, bias, proj_bias, proj_scale):
+    width = xs.shape[2]
+    length = 1024
+    heads, dim = bias.shape[0], 64
+    piece = (2, 4, 2, width // 8, width)
+    shape = jax.ShapeDtypeStruct
+    dma = pltpu.SemaphoreType.DMA
+    return pl.pallas_call(
+        forward_kernel,
+        out_shape=(
+            shape((length, width), BF),
+            shape((length // 2, width), BF),
+            shape(piece, BF),
+            shape(piece, BF),
+            shape(piece, BF),
+            shape((heads, length, dim), BF),
+            shape((heads, length, dim), BF),
+            shape((heads, length, dim), BF),
+            shape((length, 512), BF),
+            shape((heads, 1, length), F32),
+        ),
+        in_specs=[vmem()] * 8,
+        out_specs=[vmem()] * 10,
+        scratch_shapes=[
+            pltpu.VMEM((heads, dim, length), BF),
+            pltpu.VMEM((512, length), F32),
+            dma((4,)),
+            dma((4,)),
+            dma((4,)),
+            dma((4,)),
+            dma((4,)),
+            dma((4,)),
+            dma((3, 2, 7)),
+            dma((3, 2, 7)),
+        ],
+        compiler_params=pltpu.CompilerParams(
+            collective_id=1, has_side_effects=True, vmem_limit_bytes=VMEM_LIMIT
+        ),
+        name="forward",
+    )(xs, cs, *shards, bias, proj_bias, proj_scale)
+def joined_small(at, arrays, tp_count):
+    flat = jnp.concatenate([a.astype(F32).reshape(-1) for a in arrays])
+    whole = lax.all_gather(flat, ("fsdp", "tp"), axis=0)
+    whole = whole.reshape(-1, tp_count, flat.shape[0])
+    out, start = [], 0
+    for a in arrays:
+        out.append(whole[:, :, start : start + a.size].reshape(whole.shape[:2] + a.shape))
+        start += a.size
+    return out
+
+
+def list_counts(ids, blocks):
+    spots = jnp.arange(blocks)
+    near = (jnp.abs(spots[:, None] - spots[None, :]) <= 1).astype(F32)
+    ends = ((spots == 0) | (spots == blocks - 1)).astype(F32)
+    fixed = near + ends[None, :]
+    picked = jnp.sum((ids[..., None] == spots).astype(F32), axis=2)
+    counts = jnp.where((ends > 0)[None, :, None], 1.0, fixed[None] + picked)
+    logs = jnp.where(counts > 0, jnp.log(jnp.maximum(counts, 1.0)), -1e30)
+    return jnp.repeat(logs.transpose(0, 2, 1), BLK, axis=2)
+
+
+def prepare(hidden_in, rand_blocks, w_in, qv_bias, w_out, out_bias, norm_gain, norm_bias, w_up, up_bias, w_down, cotangent):
+    f, c, t = (lax.axis_index(a) for a in ("fsdp", "ctx", "tp"))
+    k, y = f % 2, f // 2
+    tp_count = lax.axis_size("tp")
+    rows, heads, wide = w_in.shape
+    dim = wide // 3
+    low = lambda a: lax.reduce_precision(a, 8, 7)
+    qv, outs, gains, shifts, ups, rand = joined_small(
+        None,
+        [low(qv_bias), low(out_bias), low(norm_gain), low(norm_bias), low(up_bias), rand_blocks],
+        tp_count,
+    )
+    slots = (k * (tp_count - 1), 1 + k * (tp_count - 3))
+    pick = lambda a: jnp.stack([lax.dynamic_index_in_dim(a, s, 0, False) for s in slots])
+    qv = pick(qv.transpose(1, 2, 0, 3).reshape(tp_count, 2, heads, dim))
+    zero = jnp.zeros_like(qv[:, 0])
+    proj_bias = jnp.stack([qv[:, 0], zero, qv[:, 1]], axis=2).reshape(2, 1, heads * wide)
+    proj_bias = jnp.pad(proj_bias, ((0, 0), (0, 0), (0, dim)))
+    one = jnp.ones((heads, 1, dim), F32)
+    proj_scale = jnp.concatenate([one * dim**-0.5, one, one], axis=1).reshape(1, heads * wide)
+    proj_scale = jnp.pad(proj_scale, ((0, 0), (0, dim)))
+    whole = lambda a: a[:, 0].transpose(1, 0, 2).reshape(2, -1)
+    outs, gains, shifts = whole(outs), whole(gains), whole(shifts)
+    ups = pick(ups.transpose(1, 0, 2).reshape(tp_count, -1))
+    ids = lax.dynamic_index_in_dim(rand, 2 * y + c, 0, False)
+    ids = pick(lax.dynamic_index_in_dim(ids, t, 1, False))
+    ids = ids.transpose(0, 2, 1, 3).reshape(2 * heads, ids.shape[1], ids.shape[3])
+    bias = list_counts(ids, ids.shape[1])
+    shard0 = jnp.concatenate([w_in.reshape(rows, heads * wide), w_out.T], axis=1).astype(BF)
+    shard1 = w_up.astype(BF)
+    shard2 = w_down.T.astype(BF)
+    xs = hidden_in.transpose(1, 0, 2)
+    cs = cotangent.transpose(1, 0, 2)
+    return xs, cs, (shard0, shard1, shard2), bias, proj_bias, proj_scale, outs, gains, shifts, ups
+ROWS = 256
+
+
+def norm_stats(value):
+    mean = jnp.mean(value, axis=-1, keepdims=True)
+    centred = value - mean
+    inverse = lax.rsqrt(jnp.mean(centred * centred, axis=-1, keepdims=True) + EPS)
+    return centred * inverse, inverse
+
+
+def gelu_both(value):
+    share = 0.5 + 0.5 * lax.erf(value * 0.7071067811865476)
+    density = jnp.exp(value * value * -0.5) * 0.3989422804014327
+    return value * share, share + value * density
+
+
+def row_sum(value):
+    return jnp.sum(value, axis=0, keepdims=True)
+
+
+class Cores:
+    def __init__(self, at, out, back, send, recv, row_send, row_recv):
+        self.at, self.out, self.back = at, out, back
+        self.send, self.recv, self.row_send, self.row_recv = send, recv, row_send, row_recv
+
+    def rows(self, half, i):
+        return pl.ds(pl.multiple_of(half * 512 + i * ROWS, ROWS), ROWS)
+
+    def part(self, stage, i):
+        return copy_to(self.out.at[i], self.back.at[i], self.send.at[stage, i], self.recv.at[stage, i], self.at.core)
+
+    def reduce(self, stage, partial, finish):
+        at = self.at
+
+        @pl.loop(0, 512 // ROWS)
+        def _(i):
+            self.out[i] = partial(self.rows(1 - at.k, i))
+            self.part(stage, i).start()
+
+        @pl.loop(0, 512 // ROWS)
+        def _(i):
+            total = partial(self.rows(at.k, i))
+            self.part(stage, i).wait_recv()
+            finish(i, self.rows(at.k, i), total + self.back[i])
+
+        @pl.loop(0, 512 // ROWS)
+        def _(i):
+            self.part(stage, i).wait_send()
+
+    def row(self, stage, ref, half, i):
+        rows = ref.at[self.rows(half, i)]
+        return copy_to(rows, rows, self.row_send.at[stage, i], self.row_recv.at[stage, i], self.at.core)
+
+    def over_rows(self, stage, ref, work):
+        at = self.at
+
+        @pl.loop(0, 512 // ROWS)
+        def _(i):
+            work(self.rows(at.k, i))
+
+        @pl.loop(0, 512 // ROWS)
+        def _(i):
+            self.row(stage, ref, 1 - at.k, i).wait_recv()
+            work(self.rows(1 - at.k, i))
+
+        @pl.loop(0, 512 // ROWS)
+        def _(i):
+            self.row(stage, ref, at.k, i).wait_send()
+
+
+def flip(dst, src):
+    @pl.loop(0, src.shape[0] // ROWS)
+    def _(r):
+        rows = pl.ds(pl.multiple_of(r * ROWS, ROWS), ROWS)
+        dst[:, rows] = src[rows, :].T
+
+
+def product(dst, slot, flipped, right):
+    n = dst.shape[2] * dst.shape[3]
+
+    @pl.loop(0, dst.shape[1])
+    def _(r):
+        rows = pl.ds(pl.multiple_of(r * n, n), n)
+        got = mm(flipped[rows, :], right())
+        dst[slot, r] = got.astype(BF).reshape(dst.shape[2:])
+
+
+def middle_kernel(
+    x_all, up_half, full0, full1, full2, mixed, outs, gains, shifts, ups,
+    layer_rows, residual, mixed_grad, grad_out, grad1, grad2, small,
+    part_out, part_back, first, first_b, act, slope, second_grad, second_b, branch_b, normed_one, inverse_one, flipped,
+    send, recv, row_send, row_recv,
+):
+    at = Place()
+    barrier = pltpu.get_barrier_semaphore()
+    pl.semaphore_signal(barrier, inc=1, device_id=at.core, device_id_type=MESH)
+    pl.semaphore_wait(barrier, 1)
+    cores = Cores(at, part_out, part_back, send, recv, row_send, row_recv)
+    width = x_all.shape[1]
+    square = lambda full, slot: full[slot].reshape(width, width)
+    out_part = lambda slot: full0[slot, :, :, :, 512:768].reshape(width, 256)
+    local = lambda i: pl.ds(pl.multiple_of(i * ROWS, ROWS), ROWS)
+    small[...] = jnp.zeros_like(small)
+
+    def tally(row, value):
+        small[row : row + 1, :] += row_sum(value)
+
+    def branch_part(rows):
+        return mm(mixed[rows, 0:256], out_part(0), NT) + mm(mixed[rows, 256:512], out_part(1), NT)
+
+    def branch_done(i, rows, total):
+        normed, inverse = norm_stats(x_all[rows, :].astype(F32) + (total + outs[0:1, :]))
+        value = normed * gains[0:1, :] + shifts[0:1, :]
+        normed_one[local(i), :] = normed
+        inverse_one[local(i), :] = inverse
+        first[local(i), :] = value
+        first_b[rows, :] = value.astype(BF)
+        cores.row(0, first_b, at.k, i).start()
+
+    cores.reduce(0, branch_part, branch_done)
+
+    def up(rows):
+        for slot in range(2):
+            inner = mm(first_b[rows, :], square(full1, slot)) + ups[slot : slot + 1, :]
+            value, slope_value = gelu_both(inner)
+            act[slot, rows, :] = value.astype(BF)
+            slope[slot, rows, :] = slope_value.astype(BF)
+
+    cores.over_rows(0, first_b, up)
+
+    def second_part(rows):
+        return mm(act[0, rows, :], square(full2, 0), NT) + mm(act[1, rows, :], square(full2, 1), NT)
+
+    def second_done(i, rows, total):
+        normed, inverse = norm_stats(first[local(i), :] + (total + outs[1:2, :]))
+        layer_rows[local(i), :] = (normed * gains[1:2, :] + shifts[1:2, :]).astype(BF)
+        upstream = up_half[local(i), :].astype(F32)
+        scaled = upstream * gains[1:2, :]
+        grad = inverse * (
+            scaled
+            - jnp.mean(scaled, axis=-1, keepdims=True)
+            - normed * jnp.mean(scaled * normed, axis=-1, keepdims=True)
+        )
+        second_grad[local(i), :] = grad
+        low = grad.astype(BF)
+        second_b[rows, :] = low
+        cores.row(1, second_b, at.k, i).start()
+        tally(1, low.astype(F32))
+        tally(3, upstream * normed)
+        tally(5, upstream)
+
+    cores.reduce(1, second_part, second_done)
+
+    def down(rows):
+        for slot in range(2):
+            grad = mm(second_b[rows, :], square(full2, slot)) * slope[slot, rows, :].astype(F32)
+            low = grad.astype(BF)
+            slope[slot, rows, :] = low
+            tally(6 + slot, low.astype(F32))
+
+    cores.over_rows(1, second_b, down)
+
+    def first_part(rows):
+        return mm(slope[0, rows, :], square(full1, 0), NT) + mm(slope[1, rows, :], square(full1, 1), NT)
+
+    def first_done(i, rows, total):
+        grad = total + second_grad[local(i), :]
+        normed = normed_one[local(i), :]
+        tally(2, grad * normed)
+        tally(4, grad)
+        scaled = grad * gains[0:1, :]
+        back = inverse_one[local(i), :] * (
+            scaled
+            - jnp.mean(scaled, axis=-1, keepdims=True)
+            - normed * jnp.mean(scaled * normed, axis=-1, keepdims=True)
+        )
+        residual[local(i), :] = back
+        low = back.astype(BF)
+        branch_b[rows, :] = low
+        cores.row(2, branch_b, at.k, i).start()
+        tally(0, low.astype(F32))
+
+    cores.reduce(2, first_part, first_done)
+
+    def mix_back(rows):
+        for slot in range(2):
+            got = mm(branch_b[rows, :], out_part(slot))
+            for i in range(3):
+                mixed_grad[slot * 3 + i, rows, :] = got[:, 64 + 64 * i : 128 + 64 * i].astype(BF)
+
+    cores.over_rows(2, branch_b, mix_back)
+
+    flip(flipped, second_b)
+    for slot in range(2):
+        product(grad2, slot, flipped, lambda: act[slot])
+    flip(flipped, first_b)
+    for slot in range(2):
+        product(grad1, slot, flipped, lambda: slope[slot])
+    flip(flipped, branch_b)
+
+    @pl.loop(0, 4)
+    def _(r):
+        rows = pl.ds(pl.multiple_of(r * 192, 192), 192)
+        grad_out[rows, :] = mm(flipped[rows, :], mixed[...])
+
+
+def middle_call(x_all, up_half, full0, full1, full2, mixed, outs, gains, shifts, ups):
+    length, width = x_all.shape
+    shape = jax.ShapeDtypeStruct
+    dma = pltpu.SemaphoreType.DMA
+    half = length // 2
+    parts = half // ROWS
+    return pl.pallas_call(
+        middle_kernel,
+        out_shape=(
+            shape((half, width), BF),
+            shape((half, width), F32),
+            shape((6, length, 64), BF),
+            shape((width, 512), F32),
+            shape(full1.shape, BF),
+            shape(full1.shape, BF),
+            shape((16, width), F32),
+        ),
+        in_specs=[vmem()] * 10,
+        out_specs=[vmem()] * 7,
+        scratch_shapes=[
+            pltpu.VMEM((parts, ROWS, width), F32),
+            pltpu.VMEM((parts, ROWS, width), F32),
+            pltpu.VMEM((half, width), F32),
+            pltpu.VMEM((length, width), BF),
+            pltpu.VMEM((2, length, width), BF),
+            pltpu.VMEM((2, length, width), BF),
+            pltpu.VMEM((half, width), F32),
+            pltpu.VMEM((length, width), BF),
+            pltpu.VMEM((length, width), BF),
+            pltpu.VMEM((half, width), F32),
+            pltpu.VMEM((half, 1), F32),
+            pltpu.VMEM((width, length), BF),
+            dma((3, parts)),
+            dma((3, parts)),
+            dma((3, parts)),
+            dma((3, parts)),
+        ],
+        compiler_params=pltpu.CompilerParams(
+            collective_id=2, has_side_effects=True, vmem_limit_bytes=VMEM_LIMIT
+        ),
+        name="middle",
+    )(x_all, up_half, full0, full1, full2, mixed, outs, gains, shifts, ups)
+class Reduce:
+    def __init__(self, at, grads, work, plane, zline, final, send, recv):
+        self.at, self.grads, self.work, self.plane, self.zline, self.final = at, grads, work, plane, zline, final
+        self.send, self.recv = send, recv
+
+    def cp(self, g, slot, kind, src, dst, device, recv_kind=None):
+        recv_kind = kind if recv_kind is None else recv_kind
+        return copy_to(src, dst, self.send.at[g, slot, kind], self.recv.at[g, slot, recv_kind], device)
+
+    def arrives(self, g, slot, kind, dst):
+        self.cp(g, slot, kind, dst, dst, self.at.core).wait_recv()
+
+    def plane_sends(self, g, slot):
+        at, grad, box = self.at, self.grads[g], self.plane.at[g, slot]
+        return (
+            self.cp(g, slot, 1, grad.at[slot, at.other, 1 - at.c], box.at[1], at.xnbr),
+            self.cp(g, slot, 3, grad.at[slot, at.other + 1, 1 - at.c], box.at[3], at.ynbr),
+            self.cp(g, slot, 0, grad.at[slot, at.pair, 1 - at.c], box.at[0], at.xnbr),
+            self.cp(g, slot, 2, grad.at[slot, at.other + 1, at.c], box.at[2], at.ynbr),
+        )
+
+    def sums(self, g, slot):
+        at, work, box = self.at, self.work.at[g, slot], self.plane.at[g, slot]
+        return (
+            self.cp(g, slot, 4, work.at[0], box.at[4], at.ynbr),
+            self.cp(g, slot, 5, work.at[1], box.at[5], at.xnbr),
+        )
+
+    def plane0(self, g):
+        for slot in range(2):
+            for copy in self.plane_sends(g, slot):
+                copy.start()
+
+    def plane1(self, g):
+        at, grad = self.at, self.grads[g]
+        for slot in range(2):
+            to_y, to_x = self.sums(g, slot)
+            for i, kind, piece, copy in (
+                (0, 1, (at.other, at.c), to_y),
+                (1, 3, (at.pair + 1, 1 - at.c), to_x),
+            ):
+                self.arrives(g, slot, kind, self.plane.at[g, slot, kind])
+                own = grad[slot, piece[0], piece[1]].astype(F32)
+                self.work[g, slot, i] = (own + self.plane[g, slot, kind].astype(F32)).astype(BF)
+                copy.start()
+
+    def ours(self, g, slot):
+        return self.work.at[g, slot, pl.ds(2, 2)]
+
+    def down(self, g, slot):
+        return self.cp(g, slot, 6, self.ours(g, slot), self.zline.at[g, slot, 0], self.at.zminus)
+
+    def upward(self, g, slot):
+        return self.cp(g, slot, 7, self.ours(g, slot), self.zline.at[g, slot, 1], self.at.zplus)
+
+    def plane2(self, g):
+        at, grad = self.at, self.grads[g]
+        for slot in range(2):
+            for kind in (0, 2, 4, 5):
+                self.arrives(g, slot, kind, self.plane.at[g, slot, kind])
+            for i, one, two in ((0, 0, 4), (1, 2, 5)):
+                self.work[g, slot, 2 + i] = (
+                    grad[slot, at.pair + i, at.c].astype(F32)
+                    + (self.plane[g, slot, one].astype(F32) + self.plane[g, slot, two].astype(F32))
+                ).astype(BF)
+
+            @pl.when(at.p == 3)
+            def _():
+                self.down(g, slot).start()
+
+            if slot == 1:
+
+                @pl.when(at.p == 0)
+                def _():
+                    self.upward(g, slot).start()
+
+    def add_line(self, g, slot, which):
+        self.arrives(g, slot, 6 + which, self.zline.at[g, slot, which])
+        for i in range(2):
+            self.work[g, slot, 2 + i] = (
+                self.work[g, slot, 2 + i].astype(F32) + self.zline[g, slot, which, i].astype(F32)
+            ).astype(BF)
+
+    def line(self, g, place):
+        at = self.at
+        for slot in range(2):
+            if place < slot:
+                continue
+
+            @pl.when(at.p == place)
+            def _():
+                self.add_line(g, slot, 0)
+                if slot == 1 and place == 1:
+                    self.add_line(g, slot, 1)
+                if place > slot:
+                    self.down(g, slot).start()
+                else:
+                    self.hand_out(g, slot)
+
+    def hands(self, g, slot):
+        at, final = self.at, self.final[g]
+        mine = self.work.at[g, slot, 2 + at.k]
+        theirs = self.work.at[g, slot, 3 - at.k]
+        return (
+            self.cp(g, slot, 8, theirs, final.at[at.c], at.core, 8),
+            self.cp(g, slot, 9, mine, final.at[at.c], at.xnbr, 9),
+            self.cp(g, slot, 10, theirs, final.at[at.c], (at.core[0], 1 - at.c, at.t), 9),
+        )
+
+    def hand_out(self, g, slot):
+        at = self.at
+        for copy in self.hands(g, slot):
+            copy.start()
+        self.final[g][at.c] = self.work[g, slot, 2 + at.k]
+
+    def finish(self, g, out):
+        at, final = self.at, self.final[g]
+
+        @pl.when(at.k != at.own_core)
+        def _():
+            self.arrives(g, at.own_slot, 8, final.at[at.c])
+
+        self.arrives(g, at.own_slot, 9, final.at[1 - at.c])
+        half = final.shape[1]
+        for i in range(2):
+            out[i * half : (i + 1) * half, :] = final[i].astype(F32)
+
+    def sent(self, g):
+        at = self.at
+        for slot in range(2):
+            for copy in (*self.plane_sends(g, slot), *self.sums(g, slot)):
+                copy.wait_send()
+
+            @pl.when(at.p > slot)
+            def _():
+                self.down(g, slot).wait_send()
+
+            if slot == 1:
+
+                @pl.when(at.p == 0)
+                def _():
+                    self.upward(g, slot).wait_send()
+
+            @pl.when(at.p == slot)
+            def _():
+                for copy in self.hands(g, slot):
+                    copy.wait_send()
+
+
+def attend_back_chunk(h, q, key, query, value, key_t, bias, lse, grad, key_sum, value_sum, query_t):
+    cols = pl.ds(pl.multiple_of(q * QCHUNK, QCHUNK), QCHUNK)
+    some = query[h, cols, :]
+    upper = grad[h, cols, :]
+    scores = mm(key[h], some, NT)
+    length = scores.shape[0]
+    shift = bias[h, :, cols] - lse[h, :, cols]
+    scores = (scores.reshape(length // BLK, BLK, QCHUNK) + shift[:, None, :]).reshape(length, QCHUNK)
+    probs = jnp.exp(scores)
+    probs_grad = mm(value[h], upper, NT)
+    inner = jnp.sum(probs * probs_grad, axis=0, keepdims=True)
+    scores_grad = (probs * (probs_grad - inner)).astype(BF)
+    value_sum[...] += mm(probs.astype(BF), upper)
+    key_sum[...] += mm(scores_grad, some)
+    query_t[:, cols] = mm(key_t[...], scores_grad)
+
+
+def backward_kernel(
+    x_all, full0, grad1, grad2, grad_out, query, key, value, lse, bias, mixed_grad, residual, layer_rows, small,
+    layer_blocks, grad_blocks, out0, out1, out2, small_out,
+    grad0, proj_grad, key_t, key_sum, value_sum, query_t, flipped, grad_rows, part_out, part_back,
+    work, plane, zline, final0, final1, final2, sum_out, sum_in,
+    lo_send, lo_recv, gi_send, gi_recv, w_send, w_recv, send, recv, small_send, small_recv,
+):
+    at = Place()
+    greet(at)
+    layer = Swap(at, layer_blocks, layer_rows, 0, lo_send, lo_recv)
+    inputs = Swap(at, grad_blocks, grad_rows, 0, gi_send, gi_recv)
+    reduce = Reduce(at, (grad0, grad1, grad2), work, plane, zline, (final0, final1, final2), w_send, w_recv)
+    cores = Cores(at, part_out, part_back, send, recv, None, None)
+    width = x_all.shape[1]
+    reduce.plane0(2)
+    reduce.plane0(1)
+    for s in range(4):
+        layer.start_out(s)
+    for slot in range(2):
+        proj_grad[slot, :, 576:640] = jnp.zeros((1024, 64), BF)
+
+    def attend(h):
+        key_t[...] = key[h].astype(F32).T.astype(BF)
+        key_sum[...] = jnp.zeros_like(key_sum)
+        value_sum[...] = jnp.zeros_like(value_sum)
+
+        @pl.loop(0, 1024 // QCHUNK)
+        def _(q):
+            attend_back_chunk(
+                h, q, key, query, value, key_t, bias, lse, mixed_grad, key_sum, value_sum, query_t
+            )
+
+        start = (h % 3) * 192
+        proj_grad[h // 3, :, start : start + 64] = (query_t[...] * 0.125).T.astype(BF)
+        proj_grad[h // 3, :, start + 64 : start + 128] = key_sum[...].astype(BF)
+        proj_grad[h // 3, :, start + 128 : start + 192] = value_sum[...].astype(BF)
+
+    attend(0)
+    reduce.plane1(2)
+    attend(1)
+    reduce.plane2(2)
+    attend(2)
+    reduce.line(2, 2)
+    reduce.plane1(1)
+    attend(3)
+    reduce.line(2, 1)
+    reduce.plane2(1)
+    attend(4)
+    reduce.line(2, 0)
+    reduce.line(1, 2)
+    attend(5)
+    reduce.line(1, 1)
+
+    flip(flipped, x_all)
+
+    @pl.loop(0, 4)
+    def _(r):
+        rows = pl.ds(pl.multiple_of(r * 192, 192), 192)
+        for slot in range(2):
+            got = mm(flipped[rows, :], proj_grad[slot])
+            out_part = grad_out[rows, slot * 256 : slot * 256 + 256]
+            grad0[slot, r, :, :, 0:512] = got[:, 0:512].astype(BF).reshape(2, 96, 512)
+            shared = got[:, 512:640] + out_part[:, 0:128]
+            grad0[slot, r, :, :, 512:640] = shared.astype(BF).reshape(2, 96, 128)
+            grad0[slot, r, :, :, 640:768] = out_part[:, 128:256].astype(BF).reshape(2, 96, 128)
+
+    reduce.plane0(0)
+
+    def in_part(rows):
+        return sum(
+            mm(proj_grad[slot, rows, :], full0[slot, :, :, :, 0:640].reshape(width, 640), NT)
+            for slot in range(2)
+        )
+
+    def in_done(i, rows, total):
+        local = pl.ds(pl.multiple_of(i * ROWS, ROWS), ROWS)
+        grad_rows[local, :] = (total + residual[local, :]).astype(BF)
+        for s in range(ROWS // 128):
+            inputs.start_out(i * (ROWS // 128) + s)
+
+    cores.reduce(0, in_part, in_done)
+    reduce.line(1, 0)
+    reduce.plane1(0)
+
+    t = at.t
+    steps = (at.xnbr, at.ynbr, (at.f, at.c, t + 1 - 2 * lax.rem(t, 2)), (at.f, at.c, lax.rem(t + 2, 4)))
+    sum_out[0] = small[...]
+    for slot in range(2):
+        sum_out[0, 8 + slot : 9 + slot, 0:640] = row_sum(proj_grad[slot].astype(F32))
+    for i, device in enumerate(steps):
+        copy = copy_to(sum_out.at[i], sum_in.at[i], small_send.at[i], small_recv.at[i], device)
+        copy.start()
+        copy.wait_recv()
+        if i < 3:
+            sum_out[i + 1] = sum_out[i] + sum_in[i]
+        else:
+            small_out[at.k] = sum_out[i] + sum_in[i]
+        copy.wait_send()
+    both = copy_to(small_out.at[at.k], small_out.at[at.k], small_send.at[4], small_recv.at[4], at.core)
+    both.start()
+
+    reduce.plane2(0)
+    reduce.line(0, 2)
+    reduce.line(0, 1)
+    reduce.line(0, 0)
+    reduce.finish(2, out2)
+    reduce.finish(1, out1)
+    reduce.finish(0, out0)
+    both.wait_send()
+    copy_to(small_out.at[1 - at.k], small_out.at[1 - at.k], small_send.at[4], small_recv.at[4], at.core).wait_recv()
+    for s in range(4):
+        layer.wait_out(s)
+        inputs.wait_out(s)
+    layer.sent()
+    inputs.sent()
+    for g in range(3):
+        reduce.sent(g)
+
+
+def backward_call(x_all, full0, grad1, grad2, grad_out, query, key, value, lse, bias, mixed_grad, residual, layer_rows, small):
+    length, width = x_all.shape
+    half = length // 2
+    shape = jax.ShapeDtypeStruct
+    dma = pltpu.SemaphoreType.DMA
+    fr = width // 4
+    return pl.pallas_call(
+        backward_kernel,
+        out_shape=(
+            shape((4, 128, width), BF),
+            shape((4, 128, width), BF),
+            shape((fr, width), F32),
+            shape((fr, width), F32),
+            shape((fr, width), F32),
+            shape((2, 16, width), F32),
+        ),
+        in_specs=[vmem()] * 14,
+        out_specs=[vmem()] * 6,
+        scratch_shapes=[
+            pltpu.VMEM(full0.shape, BF),
+            pltpu.VMEM((2, length, 640), BF),
+            pltpu.VMEM((64, length), BF),
+            pltpu.VMEM((length, 64), F32),
+            pltpu.VMEM((length, 64), F32),
+            pltpu.VMEM((64, length), F32),
+            pltpu.VMEM((width, length), BF),
+            pltpu.VMEM((half, width), BF),
+            pltpu.VMEM((half // ROWS, ROWS, width), F32),
+            pltpu.VMEM((half // ROWS, ROWS, width), F32),
+            pltpu.VMEM((3, 2, 4, fr // 2, width), BF),
+            pltpu.VMEM((3, 2, 6, fr // 2, width), BF),
+            pltpu.VMEM((3, 2, 2, 2, fr // 2, width), BF),
+            pltpu.VMEM((2, fr // 2, width), BF),
+            pltpu.VMEM((2, fr // 2, width), BF),
+            pltpu.VMEM((2, fr // 2, width), BF),
+            pltpu.VMEM((4, 16, width), F32),
+            pltpu.VMEM((4, 16, width), F32),
+            dma((4,)),
+            dma((4,)),
+            dma((4,)),
+            dma((4,)),
+            dma((3, 2, 11)),
+            dma((3, 2, 11)),
+            dma((1, half // ROWS)),
+            dma((1, half // ROWS)),
+            dma((5,)),
+            dma((5,)),
+        ],
+        compiler_params=pltpu.CompilerParams(
+            collective_id=3, has_side_effects=True, vmem_limit_bytes=VMEM_LIMIT
+        ),
+        name="backward",
+    )(x_all, full0, grad1, grad2, grad_out, query, key, value, lse, bias, mixed_grad, residual, layer_rows, small)
+
+
+def sequence_shards(*args):
+    w_in, w_out = args[2], args[4]
+    xs, cs, shards_low, bias, proj_bias, proj_scale, outs, gains, shifts, ups = prepare(*args)
+    x_all, up_half, full0, full1, full2, query, key, value, mixed, lse = forward_call(
+        xs, cs, shards_low, bias, proj_bias, proj_scale
+    )
+    layer_rows, residual, mixed_grad, grad_out, grad1, grad2, small = middle_call(
+        x_all, up_half, full0, full1, full2, mixed, outs, gains, shifts, ups
+    )
+    layer_blocks, grad_blocks, out0, out1, out2, sums = backward_call(
+        x_all, full0, grad1, grad2, grad_out, query, key, value, lse, bias, mixed_grad, residual, layer_rows, small
+    )
+    f, t = lax.axis_index("fsdp"), lax.axis_index("tp")
+    core, slot = t // 2, t + (t // 2) * (3 - 2 * t)
+    rows, heads, wide = w_in.shape
+    both = sums[0] + sums[1]
+    piece = lambda a: lax.dynamic_slice_in_dim(a, f * rows, rows, axis=a.ndim - 1)
+    vectors = piece(both[0:6])
+    used = lax.dynamic_index_in_dim(sums, core, 0, False)
+    up_grad = piece(lax.dynamic_index_in_dim(used, 6 + slot, 0, False))
+    proj = lax.dynamic_index_in_dim(used, 8 + slot, 0, False)[: heads * wide].reshape(heads, 3, wide // 3)
+    pair_bias = jnp.stack([proj[:, 0].reshape(-1), proj[:, 2].reshape(-1)])
+    pair_bias = lax.dynamic_slice_in_dim(pair_bias, f * (rows // 4), rows // 4, axis=1)
+    return (
+        layer_blocks.transpose(1, 0, 2),
+        grad_blocks.transpose(1, 0, 2),
+        out0[:, : heads * wide].reshape(rows, heads, wide),
+        pair_bias,
+        out0[:, heads * wide :].T,
+        vectors[0:2],
+        vectors[2:4],
+        vectors[4:6],
+        out1,
+        up_grad,
+        out2.T,
+    )
+
+
 def solution(mesh):
     placed = (
         P(("ctx", "tp"), "fsdp", None),
@@ -539,8 +1595,17 @@
         P("tp", "fsdp"),
         P(("ctx", "tp"), "fsdp", None),
     )
+    sizes = tuple(mesh.shape[a] for a in ("fsdp", "ctx", "tp"))
+
+    def local(*args):
+        part_rows, seqs, width = args[0].shape
+        rows, heads, wide = args[2].shape
+        whole = sizes == (4, 2, 4) and (part_rows, seqs, width) == (128, 4, 768)
+        whole = whole and (rows, heads, wide) == (192, 3, 192) and args[8].shape == (192, 768)
+        return (sequence_shards if whole else span_shards)(*args)
+
     return jax.shard_map(
-        shards,
+        local,
         mesh=mesh,
         in_specs=placed,
         out_specs=(

time: 1880 us -> 442 us (0.24)
  waiting for transfers between devices: 955 us -> 81.9 us
  local copies, waits for them, and re-layouts: 360 us -> 25.1 us
  Pallas kernels: 0 us -> 305 us
  blocking collectives: 180 us -> 0 us
  matrix products: 172 us -> 0 us
  other arithmetic: 164 us -> 9.36 us
    reduce_scatter x7 -> x0, waiting for transfers between devices: 503 us -> none  [the longest x4 418 us: rows_sum(): lax.psum_scatter(lax.dot_general(left, right, (((1,), (contract,)), ((),...]
    pallas_call x0 -> x3, Pallas kernels: none -> 305 us  [the longest x1 154 us: backward_call(): pl.pallas_call(backward_kernel, out_shape=(shape((4, 128, width), BF), sh...]
    all_gather x6 -> x0, waiting for transfers between devices: 222 us -> none  [the longest x4 206 us: rows_all(): return lax.all_gather(value, 'tp', axis=0, tiled=True)]
    dot_general x46 -> x0, matrix products: 168 us -> none  [the longest x4 22.9 us: rows_sum(): lax.dot_general(left, right, (((1,), (contract,)), ((), ())), preferred_e...]
    psum x5 -> x0, waiting for transfers between devices: 144 us -> none  [the longest x1 60.5 us: shards(): lax.psum((shares[0], shares[1], shares[2], shares[6], shares[7], shares[8...]
    all_gather x16 -> x0, blocking collectives: 130 us -> none  [the longest x8 75 us: random_pairs_for(): whole = lax.all_gather(block_group, 'ctx', axis=2, tiled=True)]
    concatenate x44 -> x1, local copies, waits for them, and re-layouts: 77.7 us -> 0.08 us  [joined_small(): flat = jnp.concatenate([a.astype(F32).reshape(-1) for a in arrays])]
    scatter-add x18 -> x0, other arithmetic: 76.3 us -> none  [the longest x4 53.1 us: random_back(): spread_grad = jnp.zeros((group, heads, blocks_all, BLK, pair_width), jnp....]
  transfers between devices with their start and end apart: 31 -> 1, of which waited for: 26 -> 1; matrix products, arithmetic and copies ran while one was open for 12% -> 1% of each run, Pallas kernels for 0% -> 0%
where the time goes in v1:
time: 442 us; the launch traced here: 436 us
  Pallas kernels  305 us (69%)
  waiting for transfers between devices  81.9 us (19%)
  local copies, waits for them, and re-layouts  25.1 us (6%)
  between operations  15.1 us (3%)
  other arithmetic  9.36 us (2%)
    pallas_call x1, Pallas kernels, backward_call(): pl.pallas_call(backward_kernel, out_shape=(shape((4, 128, width), BF), sh...  154 us
    pallas_call x1, Pallas kernels, forward_call(): pl.pallas_call(forward_kernel, out_shape=(shape((length, width), BF), sha...  108 us
    unnamed x2, waiting for transfers between devices  81.9 us
    pallas_call x1, Pallas kernels, middle_call(): pl.pallas_call(middle_kernel, out_shape=(shape((half, width), BF), shape(...  43.4 us
    unnamed x33, local copies, waits for them, and re-layouts  8.85 us
  transfers between devices with their start and end apart: 1, of which 1 were waited for; matrix products, arithmetic and copies ran while one was open for 1% of the time, Pallas kernels for 0%

profile of v1, /device:TPU:11, one launch (start us, length us, event | category | flops | bytes accessed | tf_op | source)
XLA Modules:
  0.0 436.4 jit_solution(11015300554914324837)
XLA Ops:
  7.3 0.8 convert_element_type.52
  12.2 1.2 dynamic-slice.12
  15.3 1.2 convert.8
  17.0 0.7 convert_bitcast_fusion.shard2
  17.8 0.7 convert_element_type.47.shard1
  18.6 1.3 copy_bitcast_fusion
  19.9 0.8 pad_maximum_fusion.shard0
  20.7 81.9 %all-reduce.4.cloned.1.call-done = f32[32256]{0:T(1024)} async-done(((f32[32256]{0:T(1024)}), f32[32256]{0:T(1024)}) %all-reduce.4.cloned.1.call-update) | async-done | bytes 129040
  102.6 1.0 reshape.161
  103.9 1.3 reshape.162
  106.1 1.0 reshape.163.bias
  111.2 108.0 %forward.1 = (bf16[1024,768]{1,0:T(8,128)(2,1)}, bf16[512,768]{1,0:T(8,128)(2,1)}, bf16[2,4,2,96,768]{4,3,2,1,0:T(8,128)(2,1)}, bf16[2,4,2,96,768]{4,3,2,1,0:T(8...) custom-call(bf16[4,128,768]{2,1,0:T(8,128)(2,1)} %get-tuple-element., ...), custom_call_target="tpu_custom_call" | custom-call | tf_op jit(solution)/shard_map/forward/pallas_call | solution.py:868
  219.2 43.4 %middle.1 = (bf16[512,768]{1,0:T(8,128)(2,1)}, f32[512,768]{1,0:T(8,128)}, bf16[6,1024,64]{2,1,0:T(8,128)(2,1)}, f32[768,512]{1,0:T(8,128)}, bf16[2,4,2,96,768]{...) custom-call(bf16[1024,768]{1,0:T(8,128)(2,1)} %get-tuple-element.34.x_all, ...), custom_call_target="tpu_custom_call" | custom-call | tf_op jit(solution)/shard_map/middle/pallas_call | solution.py:1169
  262.7 153.5 %backward.1 = (bf16[4,128,768]{2,1,0:T(8,128)(2,1)}, bf16[4,128,768]{2,1,0:T(8,128)(2,1)}, f32[192,768]{1,0:T(8,128)}, f32[192,768]{1,0:T(8,128)}, f32[192,768]{1,0:T(8,128)}, /*index=5*/f32[2,16,768]{2,1,0:T(8,128)}) custom-call(bf16[1024,768]{1,0:T(8,128)(2,1)} %get-tuple-element.34.x_all, bf16[2,4,2,96,768]{4,3,2,1,0:T(8,128)(2,1)} %get-tuple-element.35.full0, ...), custom_call_target="tpu_custom_call" | custom-call | tf_op jit(solution)/shard_map/backward/pallas_call | solution.py:1496
  416.2 1.1 slice.88
  417.3 1.0 slice_bitcast_fusion
  418.4 0.8 fusion.7
  421.1 1.1 copy.98
  422.2 1.5 copy.96
  423.7 1.5 copy.97
  425.2 0.8 copy.99
  426.0 1.3 dynamic_slice.58
  427.9 0.8 copy.118
  428.8 0.8 copy.119
  (90 shorter events, 13.4 us)
Async XLA Ops:
  7.2 9.8 %copy-start.4 = (f32[768,192]{0,1:T(8,128)S(1)}, f32[768,192]{0,1:T(8,128)}, u32[]{:S(2)}) copy-start(f32[768,192]{0,1:T(8,128)} %param.22) | copy-start | bytes 1769476
  7.2 10.6 %copy-start.5 = (f32[192,768]{1,0:T(8,128)S(1)}, f32[192,768]{1,0:T(8,128)}, u32[]{:S(2)}) copy-start(f32[192,768]{1,0:T(8,128)} %param.20) | copy-start | bytes 1769476
  7.2 95.4 %all-reduce.4.cloned.1.call-start = ((), (), s32[]{:S(2)}) async-start(), calls=%async_computation | async-start | bytes 262144
  14.5 0.7 copy-start.8
  15.2 1.7 copy-start.9
  15.2 3.4 copy-start.2
  15.2 3.3 copy-start.3
  416.2 6.0 %copy-start.1 = (bf16[4,128,768]{2,1,0:T(8,128)(2,1)S(1)}, bf16[4,128,768]{2,1,0:T(8,128)(2,1)}, u32[]{:S(2)}) copy-start(bf16[4,128,768]{2,1,0:T(8,128)(2,1)} %get-tuple-element.51) | copy-start | bytes 2359300
  418.4 5.3 %copy-start = (bf16[4,128,768]{2,1,0:T(8,128)(2,1)S(1)}, bf16[4,128,768]{2,1,0:T(8,128)(2,1)}, u32[]{:S(2)}) copy-start(bf16[4,128,768]{2,1,0:T(8,128)(2,1)} %get-tuple-element.52) | copy-start | bytes 2359300
  421.1 6.8 %copy-start.7 = (f32[192,768]{1,0:T(8,128)S(1)}, f32[192,768]{1,0:T(8,128)}, u32[]{:S(2)}) copy-start(f32[192,768]{1,0:T(8,128)} %get-tuple-element.142) | copy-start | bytes 1769476
  422.2 6.6 %copy-start.6 = (f32[192,768]{1,0:T(8,128)S(1)}, f32[192,768]{1,0:T(8,128)}, u32[]{:S(2)}) copy-start(f32[192,768]{1,0:T(8,128)} %get-tuple-element.56) | copy-start | bytes 1769476
Sparse Core Ops, SparseCore 0:
  15.3 87.2 all-reduce.3

commit v2 on v1

--- a/solution.py
+++ b/solution.py
@@ -571,7 +571,7 @@
     )
 
 
-def greet(at):
+def greet(at, between=lambda: None):
     barrier = pltpu.get_barrier_semaphore()
     sizes = [lax.axis_size(a) for a in ("fsdp", "ctx", "tp")]
     others = 0
@@ -586,6 +586,7 @@
                         lax.rem(at.t + m, sizes[2]),
                     )
                     pl.semaphore_signal(barrier, inc=1, device_id=device, device_id_type=MESH)
+    between()
     pl.semaphore_wait(barrier, others)
 
 
@@ -763,18 +764,152 @@
     mixed_t[spots(h), cols] = mm(value_t[h], probs)
 
 
+class Vectors:
+    def __init__(self, at, own, vec, near, ids, picked, sems):
+        self.at, self.own, self.vec, self.near, self.ids, self.picked = at, own, vec, near, ids, picked
+        self.send, self.recv = sems
+
+    def fill(self, out_bias, norm_gain, norm_bias, up_bias, qv_bias, rand):
+        at = self.at
+        size = out_bias.shape[1]
+        for i, ref in enumerate((out_bias, norm_gain, norm_bias)):
+            self.vec[at.f, 2 * i : 2 * i + 2, 0:size] = ref[...]
+        self.own[0:1, 0:size] = up_bias[...]
+        self.own[1:3, 0 : qv_bias.shape[1]] = qv_bias[...]
+        self.ids[:, :, 0 : rand.shape[2]] = rand[...].astype(F32).astype(BF)
+
+        @pl.when(at.k == at.own_core)
+        def _():
+            self.near[at.own_slot, at.f] = self.own[...]
+
+            @pl.when(at.k == at.c)
+            def _():
+                self.picked[at.own_slot] = self.ids[at.t]
+
+    def copies(self):
+        at = self.at
+        out = []
+        box = self.vec.at[at.f]
+        for i, f in enumerate((at.core[0], at.ynbr[0], lax.rem(at.core[0] + 2, 4))):
+            out.append((None, copy_to(box, box, self.send.at[i], self.recv.at[at.f], (f, at.c, at.t))))
+        for y in range(2):
+            for t in range(4):
+                f = 2 * y + at.own_core
+                copy = copy_to(
+                    self.own,
+                    self.near.at[at.own_slot, at.f],
+                    self.send.at[3 + 4 * y + t],
+                    self.recv.at[4 + 4 * at.own_slot + at.f],
+                    (f, at.c, t),
+                )
+                out.append((jnp.logical_or(f != at.f, t != at.t), copy))
+        for s in range(4):
+            f = at.pair + at.own_core
+            copy = copy_to(
+                self.ids.at[s],
+                self.picked.at[at.own_slot],
+                self.send.at[11 + s],
+                self.recv.at[12 + at.own_slot],
+                (f, at.k, s),
+            )
+            away = jnp.logical_or(f != at.f, s != at.t)
+            out.append((jnp.logical_and(at.c == at.k, away), copy))
+        return out
+
+    def each(self, act):
+        for condition, copy in self.copies():
+            if condition is None:
+                act(copy)
+            else:
+                pl.when(condition)(lambda copy=copy: act(copy))
+
+    def start(self):
+        self.each(lambda copy: copy.start())
+
+    def sent(self):
+        self.each(lambda copy: copy.wait_send())
+
+    def wait(self):
+        at = self.at
+
+        def arrives(index, dst):
+            copy_to(dst, dst, self.send.at[0], self.recv.at[index], at.core).wait_recv()
+
+        for i in range(1, 4):
+            f = lax.rem(at.f + i, 4)
+            arrives(f, self.vec.at[f])
+        for slot in range(2):
+            ours = jnp.logical_and(at.k == at.own_core, slot == at.own_slot)
+            for f in range(4):
+
+                @pl.when(jnp.logical_not(jnp.logical_and(ours, f == at.f)))
+                def _():
+                    arrives(4 + 4 * slot + f, self.near.at[slot, f])
+
+            @pl.when(jnp.logical_not(jnp.logical_and(ours, at.k == at.c)))
+            def _():
+                arrives(12 + slot, self.picked.at[slot])
+
+    def unpack(self, vec_out, ups, proj_bias, row, bias):
+        size = vec_out.shape[1] // 4
+        low = lambda a: a.astype(BF).astype(F32)
+        part = size // 4
+        for f in range(4):
+            vec_out[:, size * f : size * (f + 1)] = low(self.vec[f, :, 0:size])
+        proj_bias[...] = jnp.zeros_like(proj_bias)
+        for slot in range(2):
+            for f in range(4):
+                ups[slot : slot + 1, size * f : size * (f + 1)] = low(self.near[slot, f, 0:1, 0:size])
+                row[slot, 0:2, part * f : part * (f + 1)] = low(self.near[slot, f, 1:3, 0:part])
+            for i in range(3):
+                start = i * size
+                proj_bias[slot, :, start : start + 64] = row[slot, 0:1, 64 * i : 64 * i + 64]
+                proj_bias[slot, :, start + 128 : start + 192] = row[slot, 1:2, 64 * i : 64 * i + 64]
+        blocks, length = bias.shape[1], bias.shape[2]
+        spot = lax.broadcasted_iota(jnp.int32, (blocks, length), 0)
+        block = lax.broadcasted_iota(jnp.int32, (blocks, length), 1) // BLK
+        number = lambda mask: jnp.where(mask, 1.0, 0.0)
+        fixed = number(jnp.abs(spot - block) <= 1) + number(spot == 0) + number(spot == blocks - 1)
+        edge = jnp.logical_or(block == 0, block == blocks - 1)
+        spread_out = number(spot == block).astype(BF)
+        here = spot.astype(F32)
+        for slot in range(2):
+            ids = mm(self.picked[slot], spread_out, TN)
+            for i in range(3):
+                counts = fixed
+                for r in range(3):
+                    counts = counts + number(ids[3 * i + r : 3 * i + r + 1, :] == here)
+                counts = jnp.where(edge, 1.0, counts)
+                bias[3 * slot + i] = jnp.where(counts > 0.5, jnp.log(jnp.maximum(counts, 1.0)), -1e30)
+
+
 def forward_kernel(
-    xs, cs, shard0, shard1, shard2, bias, proj_bias, proj_scale,
-    x_all, up_half, full0, full1, full2, query, key, value, mixed, lse,
-    value_t, mixed_t,
-    xs_send, xs_recv, xc_send, xc_recv, cs_send, cs_recv, w_send, w_recv,
+    xs, cs, w_in, w_out, w_up, w_down, out_bias, norm_gain, norm_bias, up_bias, qv_bias, rand,
+    x_all, up_half, full0, full1, full2, query, key, value, mixed, lse, bias, vec_out, ups,
+    value_t, mixed_t, shard0, shard1, shard2, own, vec, near, ids, picked, proj_bias, bias_row,
+    xs_send, xs_recv, xc_send, xc_recv, cs_send, cs_recv, w_send, w_recv, v_send, v_recv,
 ):
     at = Place()
-    greet(at)
+    small = Vectors(at, own, vec, near, ids, picked, (v_send, v_recv))
+    wide = w_in.shape[2]
+
+    def pack():
+        for h in range(3):
+            shard0[:, h * wide : (h + 1) * wide] = w_in[:, h, :].astype(BF)
+        shard0[:, 3 * wide : 4 * wide] = w_out[...].T.astype(BF)
+        shard1[...] = w_up[...].astype(BF)
+        shard2[...] = w_down[...].T.astype(BF)
+        own[...] = jnp.zeros_like(own)
+        ids[...] = jnp.zeros_like(ids)
+        vec[at.f] = jnp.zeros(vec.shape[1:], F32)
+        small.fill(out_bias, norm_gain, norm_bias, up_bias, qv_bias, rand)
+
+    greet(at, pack)
     gather = Gather(at, (shard0, shard1, shard2), (full0, full1, full2), w_send, w_recv)
     tokens = Swap(at, xs, x_all, 512, xs_send, xs_recv)
     grads = Swap(at, cs, up_half, 0, cs_send, cs_recv)
     part = xs.shape[1]
+    small.start()
     tokens.start_in()
     for g in range(3):
         gather.own(g)
@@ -797,6 +932,8 @@
         to_core(s, 1 - at.k).wait_recv()
     gather.step_last(0)
 
+    small.wait()
+    small.unpack(vec_out, ups, proj_bias, bias_row, bias)
     heads = query.shape[0]
     dim = query.shape[2]
     width = x_all.shape[1]
@@ -806,11 +943,11 @@
         def _(r):
             rows = pl.ds(pl.multiple_of(r * 256, 256), 256)
             weight = full0[slot, :, :, :, 0:640].reshape(width, 640)
-            got = (mm(x_all[rows, :], weight) + proj_bias[slot]) * proj_scale[...]
+            got = mm(x_all[rows, :], weight) + proj_bias[slot]
             for i in range(heads // 2):
                 h = slot * (heads // 2) + i
                 start = i * 3 * dim
-                query[h, rows, :] = got[:, start : start + dim].astype(BF)
+                query[h, rows, :] = (got[:, start : start + dim] * dim**-0.5).astype(BF)
                 key[h, rows, :] = got[:, start + dim : start + 2 * dim].astype(BF)
                 one = got[:, start + 2 * dim : start + 3 * dim]
                 value[h, rows, :] = one.astype(BF)
@@ -848,6 +985,7 @@
     for s in range(4):
         grads.wait_in(s)
         to_core(s, at.k).wait_send()
+    small.sent()
     tokens.sent()
     grads.sent()
     for g in range(3):
@@ -858,11 +996,12 @@
     return pl.BlockSpec(memory_space=pltpu.VMEM)
 
 
-def forward_call(xs, cs, shards, bias, proj_bias, proj_scale):
+def forward_call(xs, cs, w_in, w_out, w_up, w_down, out_bias, norm_gain, norm_bias, up_bias, qv_bias, rand):
     width = xs.shape[2]
     length = 1024
-    heads, dim = bias.shape[0], 64
-    piece = (2, 4, 2, width // 8, width)
+    heads, dim = 6, 64
+    fr = width // 4
+    piece = (2, 4, 2, fr // 2, width)
     shape = jax.ShapeDtypeStruct
     dma = pltpu.SemaphoreType.DMA
     return pl.pallas_call(
@@ -878,12 +1017,25 @@
             shape((heads, length, dim), BF),
             shape((length, 512), BF),
             shape((heads, 1, length), F32),
+            shape((heads, length // BLK, length), F32),
+            shape((8, width), F32),
+            shape((2, width), F32),
         ),
-        in_specs=[vmem()] * 8,
-        out_specs=[vmem()] * 10,
+        in_specs=[vmem()] * 12,
+        out_specs=[vmem()] * 13,
         scratch_shapes=[
             pltpu.VMEM((heads, dim, length), BF),
             pltpu.VMEM((512, length), F32),
+            pltpu.VMEM((fr, width), BF),
+            pltpu.VMEM((fr, width), BF),
+            pltpu.VMEM((fr, width), BF),
+            pltpu.VMEM((8, 256), F32),
+            pltpu.VMEM((4, 8, 256), F32),
+            pltpu.VMEM((2, 4, 8, 256), F32),
+            pltpu.VMEM((4, length // BLK, 128), BF),
+            pltpu.VMEM((2, length // BLK, 128), BF),
+            pltpu.VMEM((2, 1, 640), F32),
+            pltpu.VMEM((2, 8, 256), F32),
             dma((4,)),
             dma((4,)),
             dma((4,)),
@@ -892,68 +1044,14 @@
             dma((4,)),
             dma((3, 2, 7)),
             dma((3, 2, 7)),
+            dma((15,)),
+            dma((14,)),
         ],
         compiler_params=pltpu.CompilerParams(
             collective_id=1, has_side_effects=True, vmem_limit_bytes=VMEM_LIMIT
         ),
         name="forward",
-    )(xs, cs, *shards, bias, proj_bias, proj_scale)
-def joined_small(at, arrays, tp_count):
-    flat = jnp.concatenate([a.astype(F32).reshape(-1) for a in arrays])
-    whole = lax.all_gather(flat, ("fsdp", "tp"), axis=0)
-    whole = whole.reshape(-1, tp_count, flat.shape[0])
-    out, start = [], 0
-    for a in arrays:
-        out.append(whole[:, :, start : start + a.size].reshape(whole.shape[:2] + a.shape))
-        start += a.size
-    return out
-
-
-def list_counts(ids, blocks):
-    spots = jnp.arange(blocks)
-    near = (jnp.abs(spots[:, None] - spots[None, :]) <= 1).astype(F32)
-    ends = ((spots == 0) | (spots == blocks - 1)).astype(F32)
-    fixed = near + ends[None, :]
-    picked = jnp.sum((ids[..., None] == spots).astype(F32), axis=2)
-    counts = jnp.where((ends > 0)[None, :, None], 1.0, fixed[None] + picked)
-    logs = jnp.where(counts > 0, jnp.log(jnp.maximum(counts, 1.0)), -1e30)
-    return jnp.repeat(logs.transpose(0, 2, 1), BLK, axis=2)
-
-
-def prepare(hidden_in, rand_blocks, w_in, qv_bias, w_out, out_bias, norm_gain, norm_bias, w_up, up_bias, w_down, cotangent):
-    f, c, t = (lax.axis_index(a) for a in ("fsdp", "ctx", "tp"))
-    k, y = f % 2, f // 2
-    tp_count = lax.axis_size("tp")
-    rows, heads, wide = w_in.shape
-    dim = wide // 3
-    low = lambda a: lax.reduce_precision(a, 8, 7)
-    qv, outs, gains, shifts, ups, rand = joined_small(
-        None,
-        [low(qv_bias), low(out_bias), low(norm_gain), low(norm_bias), low(up_bias), rand_blocks],
-        tp_count,
-    )
-    slots = (k * (tp_count - 1), 1 + k * (tp_count - 3))
-    pick = lambda a: jnp.stack([lax.dynamic_index_in_dim(a, s, 0, False) for s in slots])
-    qv = pick(qv.transpose(1, 2, 0, 3).reshape(tp_count, 2, heads, dim))
-    zero = jnp.zeros_like(qv[:, 0])
-    proj_bias = jnp.stack([qv[:, 0], zero, qv[:, 1]], axis=2).reshape(2, 1, heads * wide)
-    proj_bias = jnp.pad(proj_bias, ((0, 0), (0, 0), (0, dim)))
-    one = jnp.ones((heads, 1, dim), F32)
-    proj_scale = jnp.concatenate([one * dim**-0.5, one, one], axis=1).reshape(1, heads * wide)
-    proj_scale = jnp.pad(proj_scale, ((0, 0), (0, dim)))
-    whole = lambda a: a[:, 0].transpose(1, 0, 2).reshape(2, -1)
-    outs, gains, shifts = whole(outs), whole(gains), whole(shifts)
-    ups = pick(ups.transpose(1, 0, 2).reshape(tp_count, -1))
-    ids = lax.dynamic_index_in_dim(rand, 2 * y + c, 0, False)
-    ids = pick(lax.dynamic_index_in_dim(ids, t, 1, False))
-    ids = ids.transpose(0, 2, 1, 3).reshape(2 * heads, ids.shape[1], ids.shape[3])
-    bias = list_counts(ids, ids.shape[1])
-    shard0 = jnp.concatenate([w_in.reshape(rows, heads * wide), w_out.T], axis=1).astype(BF)
-    shard1 = w_up.astype(BF)
-    shard2 = w_down.T.astype(BF)
-    xs = hidden_in.transpose(1, 0, 2)
-    cs = cotangent.transpose(1, 0, 2)
-    return xs, cs, (shard0, shard1, shard2), bias, proj_bias, proj_scale, outs, gains, shifts, ups
+    )(xs, cs, w_in, w_out, w_up, w_down, out_bias, norm_gain, norm_bias, up_bias, qv_bias, rand)
 ROWS = 256
 
 
@@ -1042,7 +1140,7 @@
 
 
 def middle_kernel(
-    x_all, up_half, full0, full1, full2, mixed, outs, gains, shifts, ups,
+    x_all, up_half, full0, full1, full2, mixed, vectors, ups,
     layer_rows, residual, mixed_grad, grad_out, grad1, grad2, small,
     part_out, part_back, first, first_b, act, slope, second_grad, second_b, branch_b, normed_one, inverse_one, flipped,
     send, recv, row_send, row_recv,
@@ -1065,8 +1163,8 @@
         return mm(mixed[rows, 0:256], out_part(0), NT) + mm(mixed[rows, 256:512], out_part(1), NT)
 
     def branch_done(i, rows, total):
-        normed, inverse = norm_stats(x_all[rows, :].astype(F32) + (total + outs[0:1, :]))
-        value = normed * gains[0:1, :] + shifts[0:1, :]
+        normed, inverse = norm_stats(x_all[rows, :].astype(F32) + (total + vectors[0:1, :]))
+        value = normed * vectors[2:3, :] + vectors[4:5, :]
         normed_one[local(i), :] = normed
         inverse_one[local(i), :] = inverse
         first[local(i), :] = value
@@ -1088,10 +1186,10 @@
         return mm(act[0, rows, :], square(full2, 0), NT) + mm(act[1, rows, :], square(full2, 1), NT)
 
     def second_done(i, rows, total):
-        normed, inverse = norm_stats(first[local(i), :] + (total + outs[1:2, :]))
-        layer_rows[local(i), :] = (normed * gains[1:2, :] + shifts[1:2, :]).astype(BF)
+        normed, inverse = norm_stats(first[local(i), :] + (total + vectors[1:2, :]))
+        layer_rows[local(i), :] = (normed * vectors[3:4, :] + vectors[5:6, :]).astype(BF)
         upstream = up_half[local(i), :].astype(F32)
-        scaled = upstream * gains[1:2, :]
+        scaled = upstream * vectors[3:4, :]
         grad = inverse * (
             scaled
             - jnp.mean(scaled, axis=-1, keepdims=True)
@@ -1124,7 +1222,7 @@
         normed = normed_one[local(i), :]
         tally(2, grad * normed)
         tally(4, grad)
-        scaled = grad * gains[0:1, :]
+        scaled = grad * vectors[2:3, :]
         back = inverse_one[local(i), :] * (
             scaled
             - jnp.mean(scaled, axis=-1, keepdims=True)
@@ -1160,7 +1258,7 @@
         grad_out[rows, :] = mm(flipped[rows, :], mixed[...])
 
 
-def middle_call(x_all, up_half, full0, full1, full2, mixed, outs, gains, shifts, ups):
+def middle_call(x_all, up_half, full0, full1, full2, mixed, vectors, ups):
     length, width = x_all.shape
     shape = jax.ShapeDtypeStruct
     dma = pltpu.SemaphoreType.DMA
@@ -1177,7 +1275,7 @@
             shape(full1.shape, BF),
             shape((16, width), F32),
         ),
-        in_specs=[vmem()] * 10,
+        in_specs=[vmem()] * 8,
         out_specs=[vmem()] * 7,
         scratch_shapes=[
             pltpu.VMEM((parts, ROWS, width), F32),
@@ -1201,7 +1299,7 @@
             collective_id=2, has_side_effects=True, vmem_limit_bytes=VMEM_LIMIT
         ),
         name="middle",
-    )(x_all, up_half, full0, full1, full2, mixed, outs, gains, shifts, ups)
+    )(x_all, up_half, full0, full1, full2, mixed, vectors, ups)
 class Reduce:
     def __init__(self, at, grads, work, plane, zline, final, send, recv):
         self.at, self.grads, self.work, self.plane, self.zline, self.final = at, grads, work, plane, zline, final
@@ -1317,7 +1415,7 @@
             copy.start()
         self.final[g][at.c] = self.work[g, slot, 2 + at.k]
 
-    def finish(self, g, out):
+    def finish(self, g):
         at, final = self.at, self.final[g]
 
         @pl.when(at.k != at.own_core)
@@ -1325,9 +1423,7 @@
             self.arrives(g, at.own_slot, 8, final.at[at.c])
 
         self.arrives(g, at.own_slot, 9, final.at[1 - at.c])
-        half = final.shape[1]
-        for i in range(2):
-            out[i * half : (i + 1) * half, :] = final[i].astype(F32)
+        return final[...].astype(F32).reshape(-1, final.shape[2])
 
     def sent(self, g):
         at = self.at
@@ -1370,8 +1466,8 @@
 
 def backward_kernel(
     x_all, full0, grad1, grad2, grad_out, query, key, value, lse, bias, mixed_grad, residual, layer_rows, small,
-    layer_blocks, grad_blocks, out0, out1, out2, small_out,
-    grad0, proj_grad, key_t, key_sum, value_sum, query_t, flipped, grad_rows, part_out, part_back,
+    layer_blocks, grad_blocks, g_in, g_qv, g_out, g_outs, g_gains, g_shifts, g_up, g_ups, g_down,
+    small_out, grad0, proj_grad, key_t, key_sum, value_sum, query_t, flipped, grad_rows, part_out, part_back,
     work, plane, zline, final0, final1, final2, sum_out, sum_in,
     lo_send, lo_recv, gi_send, gi_recv, w_send, w_recv, send, recv, small_send, small_recv,
 ):
@@ -1473,11 +1569,35 @@
     reduce.line(0, 2)
     reduce.line(0, 1)
     reduce.line(0, 0)
-    reduce.finish(2, out2)
-    reduce.finish(1, out1)
-    reduce.finish(0, out0)
+    g_down[...] = reduce.finish(2).T
+    g_up[...] = reduce.finish(1)
+    got = reduce.finish(0)
+    fr = g_up.shape[0]
+    for h in range(3):
+        g_in[:, h, :] = got[:, h * fr : (h + 1) * fr]
+    g_out[...] = got[:, 3 * fr : 4 * fr].T
     both.wait_send()
     copy_to(small_out.at[1 - at.k], small_out.at[1 - at.k], small_send.at[4], small_recv.at[4], at.core).wait_recv()
+    vectors = small_out[0, 0:8, :] + small_out[1, 0:8, :]
+    used = small_out.at[at.own_core]
+    up_row = used[pl.ds(6 + at.own_slot, 1), :]
+    proj_row = used[pl.ds(8 + at.own_slot, 1), :]
+    pick = lambda j: jnp.concatenate(
+        [proj_row[:, i * fr + 64 * j : i * fr + 64 * j + 64] for i in range(3)], axis=1
+    )
+    pair_rows = jnp.concatenate([pick(0), pick(2)], axis=0)
+    part = fr // 4
+    for f in range(4):
+
+        @pl.when(at.f == f)
+        def _():
+            piece = vectors[:, f * fr : (f + 1) * fr]
+            g_outs[...] = piece[0:2]
+            g_gains[...] = piece[2:4]
+            g_shifts[...] = piece[4:6]
+            g_ups[...] = up_row[:, f * fr : (f + 1) * fr]
+            g_qv[...] = pair_rows[:, f * part : (f + 1) * part]
+
     for s in range(4):
         layer.wait_out(s)
         inputs.wait_out(s)
@@ -1498,14 +1618,20 @@
         out_shape=(
             shape((4, 128, width), BF),
             shape((4, 128, width), BF),
+            shape((fr, 3, fr), F32),
+            shape((2, fr // 4), F32),
+            shape((fr, fr), F32),
+            shape((2, fr), F32),
+            shape((2, fr), F32),
+            shape((2, fr), F32),
             shape((fr, width), F32),
-            shape((fr, width), F32),
-            shape((fr, width), F32),
-            shape((2, 16, width), F32),
+            shape((1, fr), F32),
+            shape((width, fr), F32),
         ),
         in_specs=[vmem()] * 14,
-        out_specs=[vmem()] * 6,
+        out_specs=[vmem()] * 11,
         scratch_shapes=[
+            pltpu.VMEM((2, 16, width), F32),
             pltpu.VMEM(full0.shape, BF),
             pltpu.VMEM((2, length, 640), BF),
             pltpu.VMEM((64, length), BF),
@@ -1542,42 +1668,21 @@
     )(x_all, full0, grad1, grad2, grad_out, query, key, value, lse, bias, mixed_grad, residual, layer_rows, small)
 
 
-def sequence_shards(*args):
-    w_in, w_out = args[2], args[4]
-    xs, cs, shards_low, bias, proj_bias, proj_scale, outs, gains, shifts, ups = prepare(*args)
-    x_all, up_half, full0, full1, full2, query, key, value, mixed, lse = forward_call(
-        xs, cs, shards_low, bias, proj_bias, proj_scale
+def sequence_shards(hidden_in, rand_blocks, w_in, qv_bias, w_out, out_bias, norm_gain, norm_bias, w_up, up_bias, w_down, cotangent):
+    xs = hidden_in.transpose(1, 0, 2)
+    cs = cotangent.transpose(1, 0, 2)
+    rand = rand_blocks.reshape(rand_blocks.shape[:2] + (-1,))
+    x_all, up_half, full0, full1, full2, query, key, value, mixed, lse, bias, vectors, ups = forward_call(
+        xs, cs, w_in, w_out, w_up, w_down, out_bias, norm_gain, norm_bias, up_bias[None], qv_bias, rand
     )
     layer_rows, residual, mixed_grad, grad_out, grad1, grad2, small = middle_call(
-        x_all, up_half, full0, full1, full2, mixed, outs, gains, shifts, ups
-    )
-    layer_blocks, grad_blocks, out0, out1, out2, sums = backward_call(
+        x_all, up_half, full0, full1, full2, mixed, vectors, ups
+    )
+    layer_blocks, grad_blocks, *grads = backward_call(
         x_all, full0, grad1, grad2, grad_out, query, key, value, lse, bias, mixed_grad, residual, layer_rows, small
     )
-    f, t = lax.axis_index("fsdp"), lax.axis_index("tp")
-    core, slot = t // 2, t + (t // 2) * (3 - 2 * t)
-    rows, heads, wide = w_in.shape
-    both = sums[0] + sums[1]
-    piece = lambda a: lax.dynamic_slice_in_dim(a, f * rows, rows, axis=a.ndim - 1)
-    vectors = piece(both[0:6])
-    used = lax.dynamic_index_in_dim(sums, core, 0, False)
-    up_grad = piece(lax.dynamic_index_in_dim(used, 6 + slot, 0, False))
-    proj = lax.dynamic_index_in_dim(used, 8 + slot, 0, False)[: heads * wide].reshape(heads, 3, wide // 3)
-    pair_bias = jnp.stack([proj[:, 0].reshape(-1), proj[:, 2].reshape(-1)])
-    pair_bias = lax.dynamic_slice_in_dim(pair_bias, f * (rows // 4), rows // 4, axis=1)
-    return (
-        layer_blocks.transpose(1, 0, 2),
-        grad_blocks.transpose(1, 0, 2),
-        out0[:, : heads * wide].reshape(rows, heads, wide),
-        pair_bias,
-        out0[:, heads * wide :].T,
-        vectors[0:2],
-        vectors[2:4],
-        vectors[4:6],
-        out1,
-        up_grad,
-        out2.T,
-    )
+    grads[7] = grads[7][0]
+    return (layer_blocks.transpose(1, 0, 2), grad_blocks.transpose(1, 0, 2), *grads)
 
 
 def solution(mesh):

time: 442 us -> 326 us (0.74)
  waiting for transfers between devices: 81.9 us -> 0 us
  between operations: 15.1 us -> 0.75 us
  other arithmetic: 9.36 us -> 0 us
  local copies, waits for them, and re-layouts: 25.1 us -> 17 us
    unnamed x2 -> x0, waiting for transfers between devices: 81.9 us -> none
    unnamed x33 -> x39, local copies, waits for them, and re-layouts: 8.85 us -> 14.1 us
    reshape x21 -> x1, local copies, waits for them, and re-layouts: 6.85 us -> 1.58 us  [sequence_shards(): rand = rand_blocks.reshape(rand_blocks.shape[:2] + (-1,))]
  transfers between devices with their start and end apart: 1 -> 0, of which waited for: 1 -> 0; matrix products, arithmetic and copies ran while one was open for 1% -> 0% of each run, Pallas kernels for 0% -> 0%
where the time goes in v2:
time: 326 us; the launch traced here: 322 us
  Pallas kernels  304 us (93%)
  local copies, waits for them, and re-layouts  17 us (5%)
    pallas_call x1, Pallas kernels, backward_call(): pl.pallas_call(backward_kernel, out_shape=(shape((4, 128, width), BF), sh...  152 us
    pallas_call x1, Pallas kernels, forward_call(): pl.pallas_call(forward_kernel, out_shape=(shape((length, width), BF), sha...  109 us
    pallas_call x1, Pallas kernels, middle_call(): pl.pallas_call(middle_kernel, out_shape=(shape((half, width), BF), shape(...  43.4 us
    unnamed x39, local copies, waits for them, and re-layouts  14.1 us

profile of v2, /device:TPU:11, one launch (start us, length us, event | category | flops | bytes accessed | tf_op | source)
XLA Modules:
  0.0 321.8 jit_solution(33202597103349916)
XLA Ops:
  0.6 0.0 copy-start.1
  0.7 0.0 copy-start.6
  0.7 0.0 copy-start.2
  0.7 1.6 copy.36.rand
  2.3 2.4 copy.34.w_in
  4.6 1.2 copy.35.w_down
  5.8 1.3 copy_bitcast_fusion
  7.1 108.8 %forward.1 = (bf16[1024,768]{1,0:T(8,128)(2,1)}, bf16[512,768]{1,0:T(8,128)(2,1)}, bf16[2,4,2,96,768]{4,3,2,1,0:T(8,128)(2,1)}, bf16[2,4,2,96,768]{4,3,2,1,0:T(8...) custom-call(bf16[4,128,768]{2,1,0:T(8,128)(2,1)} %get-tuple-element., ...), custom_call_target="tpu_custom_call" | custom-call | tf_op jit(solution)/shard_map/forward/pallas_call | solution.py:1007
  115.9 43.4 %middle.1 = (bf16[512,768]{1,0:T(8,128)(2,1)}, f32[512,768]{1,0:T(8,128)}, bf16[6,1024,64]{2,1,0:T(8,128)(2,1)}, f32[768,512]{1,0:T(8,128)}, bf16[2,4,2,96,768]{...) custom-call(bf16[1024,768]{1,0:T(8,128)(2,1)} %get-tuple-element.42.x_all, ...), custom_call_target="tpu_custom_call" | custom-call | tf_op jit(solution)/shard_map/middle/pallas_call | solution.py:1267
  159.3 151.8 %backward.1 = (bf16[4,128,768]{2,1,0:T(8,128)(2,1)}, bf16[4,128,768]{2,1,0:T(8,128)(2,1)}, f32[192,3,192]{2,1,0:T(4,128)}, f32[2,48]{1,0:T(2,128)}, f32[192,192]...) custom-call(bf16[1024,768]{1,0:T(8,128)(2,1)} %get-tuple-element.42., ...), custom_call_target="tpu_custom_call" | custom-call | tf_op jit(solution)/shard_map/backward/pallas_call | solution.py:1616
  311.2 2.7 copy.37
  314.0 1.5 copy.38
  315.5 0.9 copy.39
  316.4 0.0 copy-done.3
  316.4 1.1 copy.40
  317.5 0.0 copy-done.12
  317.5 0.6 copy.50
  318.0 0.7 copy.51
  318.7 0.6 copy.52
  319.3 0.6 copy.53
  319.9 0.6 copy.54
  320.5 0.0 copy-done.5
  320.5 0.8 copy.55
  321.3 0.6 copy.56
  (20 shorter events, 0.0 us)
Async XLA Ops:
  0.6 5.1 %copy-start.1 = (bf16[128,4,768]{2,1,0:T(4,128)(2,1)S(1)}, bf16[128,4,768]{2,1,0:T(4,128)(2,1)}, u32[]{:S(2)}) copy-start(bf16[128,4,768]{2,1,0:T(4,128)(2,1)} %param.23) | copy-start | bytes 2359300
  0.7 4.0 %copy-start.6 = (f32[768,192]{0,1:T(8,128)S(1)}, f32[768,192]{0,1:T(8,128)}, u32[]{:S(2)}) copy-start(f32[768,192]{0,1:T(8,128)} %param.22) | copy-start | bytes 1769476
  0.7 5.1 %copy-start.2 = (bf16[128,4,768]{2,1,0:T(4,128)(2,1)S(1)}, bf16[128,4,768]{2,1,0:T(4,128)(2,1)}, u32[]{:S(2)}) copy-start(bf16[128,4,768]{2,1,0:T(4,128)(2,1)} %param.12) | copy-start | bytes 2359300
  311.2 2.8 copy-start
  311.2 4.2 %copy-start.4 = (f32[192,3,192]{2,1,0:T(4,128)S(1)}, f32[192,3,192]{2,1,0:T(4,128)}, u32[]{:S(2)}) copy-start(f32[192,3,192]{2,1,0:T(4,128)} %get-tuple-element.86) | copy-start | bytes 1327108
  313.9 2.5 copy-start.3
  315.4 2.0 copy-start.12
  315.4 2.6 copy-start.7
  315.4 3.3 %copy-start.10 = (f32[2,192]{1,0:T(2,128)S(1)}, f32[2,192]{1,0:T(2,128)}, u32[]{:S(2)}) copy-start(f32[2,192]{1,0:T(2,128)} %get-tuple-element.113) | copy-start | bytes 4612
  315.5 3.9 %copy-start.9 = (f32[2,192]{1,0:T(2,128)S(1)}, f32[2,192]{1,0:T(2,128)}, u32[]{:S(2)}) copy-start(f32[2,192]{1,0:T(2,128)} %get-tuple-element.114) | copy-start | bytes 4612
  315.5 4.4 %copy-start.8 = (f32[2,192]{1,0:T(2,128)S(1)}, f32[2,192]{1,0:T(2,128)}, u32[]{:S(2)}) copy-start(f32[2,192]{1,0:T(2,128)} %get-tuple-element.115) | copy-start | bytes 4612
  315.5 5.0 %copy-start.5 = (f32[192,768]{1,0:T(8,128)S(1)}, f32[192,768]{1,0:T(8,128)}, u32[]{:S(2)}) copy-start(f32[192,768]{1,0:T(8,128)} %get-tuple-element.116) | copy-start | bytes 1769476
  316.4 4.9 %copy-start.11 = (f32[1,192]{1,0:T(1,128)S(1)}, f32[1,192]{1,0:T(1,128)}, u32[]{:S(2)}) copy-start(f32[1,192]{1,0:T(1,128)} %get-tuple-element.71) | copy-start | bytes 2308

commit v3 on v0

--- a/solution.py
+++ b/solution.py
@@ -1,6 +1,8 @@
 import jax
 import jax.numpy as jnp
 from jax import lax
+from jax.experimental import pallas as pl
+from jax.experimental.pallas import tpu as pltpu
 from jax.sharding import PartitionSpec as P
 
 BLK = 64
@@ -181,7 +183,7 @@
     return (query_grad, window_grad, global_grad, random_grad)
 
 
-def shards(
+def span_shards(
     hidden_in,
     rand_blocks,
     w_in,
@@ -283,8 +285,6 @@
     table = table.transpose(0, 1, 2, 4, 3).reshape(units, ctx_count)
     mine = lax.dynamic_index_in_dim(table, ctx_place, 1, keepdims=False)
     mine_groups = mine.reshape(steps, group, heads, picks, per_dev)
-    seq_pick = jnp.arange(group)[:, None, None, None]
-    head_pick = jnp.arange(heads)[None, :, None, None]
     block_index = ctx_place * per_dev + jnp.arange(per_dev)
     present = jnp.concatenate(
         [
@@ -299,7 +299,10 @@
 
     def random_pairs_for(block_group, id_group):
         whole = lax.all_gather(block_group, "ctx", axis=2, tiled=True)
-        return whole[seq_pick, head_pick, id_group]
+        chosen = jax.nn.one_hot(id_group, blocks_all, dtype=jnp.bfloat16)
+        return jnp.einsum(
+            "shpqb,shbke->shpqke", chosen, whole, preferred_element_type=jnp.float32
+        ).astype(jnp.bfloat16)
 
     query_groups = split_groups(query_heads, steps, group)
     pad_groups = split_groups(window_pad, steps, group)
@@ -377,10 +380,9 @@
     )
 
     def random_back(random_grad, id_group):
-        spread_grad = (
-            jnp.zeros((group, heads, blocks_all, BLK, pair_width), jnp.float32)
-            .at[seq_pick, head_pick, id_group]
-            .add(random_grad)
+        chosen = jax.nn.one_hot(id_group, blocks_all, dtype=jnp.float32)
+        spread_grad = jnp.einsum(
+            "shpqb,shpqke->shbke", chosen, random_grad, precision=lax.Precision.HIGHEST
         )
         return lax.psum_scatter(
             spread_grad.astype(jnp.bfloat16), "ctx", scatter_dimension=2, tiled=True
@@ -524,6 +526,1178 @@
     )
 
 
+MESH = pl.DeviceIdType.MESH
+BF = jnp.bfloat16
+F32 = jnp.float32
+NT = (((1,), (1,)), ((), ()))
+NN = (((1,), (0,)), ((), ()))
+TN = (((0,), (0,)), ((), ()))
+VMEM_LIMIT = 60 * 2**20
+
+
+def mm(left, right, dims=NN):
+    return lax.dot_general(left, right, dims, preferred_element_type=F32)
+
+
+class Place:
+    def __init__(self):
+        self.f = lax.axis_index("fsdp")
+        self.c = lax.axis_index("ctx")
+        self.t = lax.axis_index("tp")
+        f, c, t = self.f, self.c, self.t
+        self.k = k = lax.rem(f, 2)
+        self.y = y = f // 2
+        self.p = t + k * (3 - 2 * t)
+        self.core = (f + 1 - 2 * k, c, t)
+        self.xnbr = (f, 1 - c, t)
+        self.ynbr = (lax.rem(f + 2, 4), c, t)
+        self.zplus = (f, c, t + 1 - 2 * k)
+        self.zminus = (f, c, t - 1 + 2 * k)
+        self.own_core = t // 2
+        self.own_slot = t + (t // 2) * (3 - 2 * t)
+        self.pair = 2 * y
+        self.other = 2 - 2 * y
+
+    def swap(self, s):
+        return (2 * self.y + self.c, self.k, s)
+
+    def swap_is_self(self, s):
+        return jnp.logical_and(self.k == self.c, self.t == s)
+
+
+def copy_to(src, dst, send, recv, device):
+    return pltpu.make_async_remote_copy(
+        src_ref=src, dst_ref=dst, send_sem=send, recv_sem=recv, device_id=device, device_id_type=MESH
+    )
+
+
+def greet(at, between=lambda: None):
+    barrier = pltpu.get_barrier_semaphore()
+    sizes = [lax.axis_size(a) for a in ("fsdp", "ctx", "tp")]
+    others = 0
+    for i in range(sizes[0]):
+        for j in range(sizes[1]):
+            for m in range(sizes[2]):
+                if i or j or m:
+                    others += 1
+                    device = (
+                        lax.rem(at.f + i, sizes[0]),
+                        lax.rem(at.c + j, sizes[1]),
+                        lax.rem(at.t + m, sizes[2]),
+                    )
+                    pl.semaphore_signal(barrier, inc=1, device_id=device, device_id_type=MESH)
+    between()
+    pl.semaphore_wait(barrier, others)
+
+
+class Gather:
+    def __init__(self, at, shards, full, send, recv, tall):
+        self.at, self.shards, self.full, self.send, self.recv, self.tall = at, shards, full, send, recv, tall
+
+    def own(self, g):
+        at, full, shard = self.at, self.full[g], self.shards[g]
+        half = shard.shape[0] // 2
+        rows = pl.ds(pl.multiple_of(at.c * half, half), half)
+
+        @pl.when(at.k == at.own_core)
+        def _():
+            full[at.own_slot, at.f, at.c] = shard[rows, :]
+
+        @pl.when(at.k != at.own_core)
+        def _():
+            self.cp(g, at.own_slot, 0, shard.at[rows], full.at[at.own_slot, at.f, at.c], at.core).start()
+
+    def cp(self, g, slot, kind, src, dst, device):
+        return copy_to(src, dst, self.send.at[g, slot, kind], self.recv.at[g, slot, kind], device)
+
+    def arrives(self, g, slot, kind, dst):
+        self.cp(g, slot, kind, dst, dst, self.at.core).wait_recv()
+
+    def ours(self, g, slot, f, c):
+        return self.full[g].at[slot, pl.ds(f, 2), c]
+
+    def step_z(self, g, turn):
+        at, full = self.at, self.full[g]
+        first = (at.p + 2) // 3
+        slot = first if turn == 0 else 1 - first
+        piece = self.ours(g, slot, at.pair, at.c)
+
+        @pl.when(at.p == slot)
+        def _():
+            self.arrives(g, slot, 0, full.at[slot, at.core[0], at.c])
+
+        @pl.when(at.p > slot)
+        def _():
+            self.arrives(g, slot, 1, piece)
+
+        @pl.when(at.p < slot)
+        def _():
+            self.arrives(g, slot, 2, piece)
+
+        @pl.when(jnp.logical_and(at.p >= slot, at.p < 3))
+        def _():
+            self.cp(g, slot, 1, piece, piece, at.zplus).start()
+
+        @pl.when(jnp.logical_and(at.p == 1, slot == 1))
+        def _():
+            self.cp(g, slot, 2, piece, piece, at.zminus).start()
+
+        self.cp(g, slot, 3, piece, piece, at.ynbr).start()
+        self.cp(g, slot, 4, piece, piece, at.xnbr).start()
+
+    def relays(self, g, slot):
+        at, full = self.at, self.full[g]
+        if g in self.tall:
+            piece = self.ours(g, slot, at.pair, 1 - at.c)
+            return (self.cp(g, slot, 6, piece, piece, at.ynbr),)
+        even = full.at[slot, at.other, at.c]
+        odd = full.at[slot, at.pair + 1, 1 - at.c]
+        return self.cp(g, slot, 6, odd, odd, at.ynbr), self.cp(g, slot, 5, even, even, at.xnbr)
+
+    def step_relay(self, g, turn):
+        at = self.at
+        first = (at.p + 2) // 3
+        slot = first if turn == 0 else 1 - first
+        copies = self.relays(g, slot)
+        self.arrives(g, slot, 4, self.ours(g, slot, at.pair, 1 - at.c))
+        copies[0].start()
+        self.arrives(g, slot, 3, self.ours(g, slot, at.other, at.c))
+        if g not in self.tall:
+            copies[1].start()
+
+    def step_last(self, g):
+        at, full = self.at, self.full[g]
+        for slot in range(2):
+            if g in self.tall:
+                self.arrives(g, slot, 6, self.ours(g, slot, at.other, 1 - at.c))
+            else:
+                self.arrives(g, slot, 5, full.at[slot, at.other, 1 - at.c])
+                self.arrives(g, slot, 6, full.at[slot, at.other + 1, 1 - at.c])
+
+    def sent(self, g):
+        at, full = self.at, self.full[g]
+
+        def left(slot, kind, src):
+            self.cp(g, slot, kind, src, src, at.core).wait_send()
+
+        @pl.when(at.k != at.own_core)
+        def _():
+            left(at.own_slot, 0, full.at[at.own_slot, at.f, at.c])
+
+        for slot in range(2):
+            piece = self.ours(g, slot, at.pair, at.c)
+
+            @pl.when(jnp.logical_and(at.p >= slot, at.p < 3))
+            def _():
+                left(slot, 1, piece)
+
+            if slot == 1:
+
+                @pl.when(at.p == 1)
+                def _():
+                    left(slot, 2, piece)
+
+            left(slot, 3, piece)
+            left(slot, 4, piece)
+            for copy in self.relays(g, slot):
+                copy.wait_send()
+
+
+class Swap:
+    def __init__(self, at, blocks, rows, base, send, recv):
+        self.at, self.blocks, self.rows, self.base, self.send, self.recv = at, blocks, rows, base, send, recv
+        self.n = blocks.shape[1]
+
+    def span(self, s, base):
+        return pl.ds(pl.multiple_of(base + s * self.n, self.n), self.n)
+
+    def start_in(self):
+        at = self.at
+        there = self.rows.at[self.span(at.t, self.base * at.c)]
+        for s in range(4):
+
+            @pl.when(at.swap_is_self(s))
+            def _():
+                here = self.rows.at[self.span(s, self.base * at.k)]
+                pltpu.make_async_copy(self.blocks.at[s], here, self.recv.at[s]).start()
+
+            @pl.when(jnp.logical_not(at.swap_is_self(s)))
+            def _():
+                copy_to(self.blocks.at[s], there, self.send.at[s], self.recv.at[at.t], at.swap(s)).start()
+
+    def wait_in(self, s):
+        at = self.at
+        here = self.rows.at[self.span(s, self.base * at.k)]
+
+        @pl.when(jnp.logical_not(at.swap_is_self(s)))
+        def _():
+            copy_to(here, here, self.send.at[s], self.recv.at[s], at.core).wait_recv()
+
+        @pl.when(at.swap_is_self(s))
+        def _():
+            pltpu.make_async_copy(self.blocks.at[s], here, self.recv.at[s]).wait()
+
+    def start_out(self, s):
+        at = self.at
+        here = self.rows.at[self.span(s, self.base * at.k)]
+
+        @pl.when(at.swap_is_self(s))
+        def _():
+            pltpu.make_async_copy(here, self.blocks.at[s], self.send.at[s]).start()
+
+        @pl.when(jnp.logical_not(at.swap_is_self(s)))
+        def _():
+            copy_to(here, self.blocks.at[at.t], self.send.at[s], self.recv.at[at.t], at.swap(s)).start()
+
+    def wait_out(self, s):
+        at = self.at
+
+        @pl.when(jnp.logical_not(at.swap_is_self(s)))
+        def _():
+            copy_to(self.blocks.at[s], self.blocks.at[s], self.send.at[s], self.recv.at[s], at.core).wait_recv()
+
+    def sent(self, outward=False):
+        at = self.at
+        for s in range(4):
+
+            @pl.when(jnp.logical_not(at.swap_is_self(s)))
+            def _():
+                here = self.rows.at[self.span(s, self.base * at.k)] if outward else self.blocks.at[s]
+                copy_to(here, here, self.send.at[s], self.recv.at[s], at.core).wait_send()
+
+            if outward:
+
+                @pl.when(at.swap_is_self(s))
+                def _():
+                    here = self.rows.at[self.span(s, self.base * at.k)]
+                    pltpu.make_async_copy(here, self.blocks.at[s], self.send.at[s]).wait()
+ROWS = 256
+
+
+def norm_stats(value):
+    mean = jnp.mean(value, axis=-1, keepdims=True)
+    centred = value - mean
+    inverse = lax.rsqrt(jnp.mean(centred * centred, axis=-1, keepdims=True) + EPS)
+    return centred * inverse, inverse
+
+
+def gelu_both(value):
+    share = 0.5 + 0.5 * lax.erf(value * 0.7071067811865476)
+    density = jnp.exp(value * value * -0.5) * 0.3989422804014327
+    return value * share, share + value * density
+
+
+def row_sum(value):
+    return jnp.sum(value, axis=0, keepdims=True)
+
+
+class Cores:
+    def __init__(self, at, out, back, send, recv, row_send, row_recv):
+        self.at, self.out, self.back = at, out, back
+        self.send, self.recv, self.row_send, self.row_recv = send, recv, row_send, row_recv
+
+    def rows(self, half, i):
+        return pl.ds(pl.multiple_of(half * 512 + i * ROWS, ROWS), ROWS)
+
+    def part(self, stage, i):
+        return copy_to(self.out.at[i], self.back.at[i], self.send.at[stage, i], self.recv.at[stage, i], self.at.core)
+
+    def reduce(self, stage, partial, finish):
+        at = self.at
+
+        @pl.loop(0, 512 // ROWS)
+        def _(i):
+            self.out[i] = partial(self.rows(1 - at.k, i))
+            self.part(stage, i).start()
+
+        @pl.loop(0, 512 // ROWS)
+        def _(i):
+            total = partial(self.rows(at.k, i))
+            self.part(stage, i).wait_recv()
+            finish(i, self.rows(at.k, i), total + self.back[i])
+
+        @pl.loop(0, 512 // ROWS)
+        def _(i):
+            self.part(stage, i).wait_send()
+
+    def row(self, stage, ref, half, i):
+        rows = ref.at[self.rows(half, i)]
+        return copy_to(rows, rows, self.row_send.at[stage, i], self.row_recv.at[stage, i], self.at.core)
+
+    def over_rows(self, stage, ref, work):
+        at = self.at
+
+        @pl.loop(0, 512 // ROWS)
+        def _(i):
+            work(self.rows(at.k, i))
+
+        @pl.loop(0, 512 // ROWS)
+        def _(i):
+            self.row(stage, ref, 1 - at.k, i).wait_recv()
+            work(self.rows(1 - at.k, i))
+
+        @pl.loop(0, 512 // ROWS)
+        def _(i):
+            self.row(stage, ref, at.k, i).wait_send()
+
+
+def flip(dst, src):
+    @pl.loop(0, src.shape[0] // ROWS)
+    def _(r):
+        rows = pl.ds(pl.multiple_of(r * ROWS, ROWS), ROWS)
+        dst[:, rows] = src[rows, :].T
+
+
+def product(dst, slot, flipped, right):
+    n = dst.shape[2] * dst.shape[3]
+
+    @pl.loop(0, dst.shape[1])
+    def _(r):
+        rows = pl.ds(pl.multiple_of(r * n, n), n)
+        got = mm(flipped[rows, :], right())
+        dst[slot, r] = got.astype(BF).reshape(dst.shape[2:])
+
+
+def vmem():
+    return pl.BlockSpec(memory_space=pltpu.VMEM)
+
+
+QCHUNK = 256
+
+
+def attend_chunk(h, q, key, query, value_t, bias, lse, mixed_t):
+    cols = pl.ds(pl.multiple_of(q * QCHUNK, QCHUNK), QCHUNK)
+    scores = mm(key[h], query[h, cols, :], NT)
+    length = scores.shape[0]
+    scores = (
+        scores.reshape(length // BLK, BLK, QCHUNK) + bias[h, :, cols][:, None, :]
+    ).reshape(length, QCHUNK)
+    top = jnp.max(scores, axis=0, keepdims=True)
+    weights = jnp.exp(scores - top)
+    total = jnp.sum(weights, axis=0, keepdims=True)
+    probs = (weights * (1.0 / total)).astype(BF)
+    lse[h, :, cols] = top + jnp.log(total)
+    mixed_t[:, cols] = mm(value_t[...], probs).astype(BF)
+
+
+class Vectors:
+    def __init__(self, at, own, vec, near, ids, picked, sems):
+        self.at, self.own, self.vec, self.near, self.ids, self.picked = at, own, vec, near, ids, picked
+        self.send, self.recv = sems
+
+    def fill(self, out_bias, norm_gain, norm_bias, up_bias, qv_bias, rand):
+        at = self.at
+        size = out_bias.shape[1]
+        for i, ref in enumerate((out_bias, norm_gain, norm_bias)):
+            self.vec[at.f, 2 * i : 2 * i + 2, 0:size] = ref[...]
+        self.own[0:1, 0:size] = up_bias[...]
+        self.own[1:3, 0 : qv_bias.shape[1]] = qv_bias[...]
+        for h in range(3):
+            for r in range(3):
+                self.ids[:, 3 * h + r, 0 : rand.shape[3]] = rand[h, r].astype(F32)
+
+        @pl.when(at.k == at.own_core)
+        def _():
+            self.near[at.own_slot, at.f] = self.own[...]
+
+            @pl.when(at.k == at.c)
+            def _():
+                self.picked[at.own_slot] = self.ids[at.t]
+
+    def copies(self):
+        at = self.at
+        out = []
+        box = self.vec.at[at.f]
+        for i, f in enumerate((at.core[0], at.ynbr[0], lax.rem(at.core[0] + 2, 4))):
+            out.append((None, copy_to(box, box, self.send.at[i], self.recv.at[at.f], (f, at.c, at.t))))
+        for y in range(2):
+            for t in range(4):
+                f = 2 * y + at.own_core
+                copy = copy_to(
+                    self.own,
+                    self.near.at[at.own_slot, at.f],
+                    self.send.at[3 + 4 * y + t],
+                    self.recv.at[4 + 4 * at.own_slot + at.f],
+                    (f, at.c, t),
+                )
+                out.append((jnp.logical_or(f != at.f, t != at.t), copy))
+        for s in range(4):
+            f = at.pair + at.own_core
+            copy = copy_to(
+                self.ids.at[s],
+                self.picked.at[at.own_slot],
+                self.send.at[11 + s],
+                self.recv.at[12 + at.own_slot],
+                (f, at.k, s),
+            )
+            away = jnp.logical_or(f != at.f, s != at.t)
+            out.append((jnp.logical_and(at.c == at.k, away), copy))
+        return out
+
+    def each(self, act):
+        for condition, copy in self.copies():
+            if condition is None:
+                act(copy)
+            else:
+                pl.when(condition)(lambda copy=copy: act(copy))
+
+    def start(self):
+        self.each(lambda copy: copy.start())
+
+    def sent(self):
+        self.each(lambda copy: copy.wait_send())
+
+    def wait(self):
+        at = self.at
+
+        def arrives(index, dst):
+            copy_to(dst, dst, self.send.at[0], self.recv.at[index], at.core).wait_recv()
+
+        for i in range(1, 4):
+            f = lax.rem(at.f + i, 4)
+            arrives(f, self.vec.at[f])
+        for slot in range(2):
+            ours = jnp.logical_and(at.k == at.own_core, slot == at.own_slot)
+            for f in range(4):
+
+                @pl.when(jnp.logical_not(jnp.logical_and(ours, f == at.f)))
+                def _():
+                    arrives(4 + 4 * slot + f, self.near.at[slot, f])
+
+            @pl.when(jnp.logical_not(jnp.logical_and(ours, at.k == at.c)))
+            def _():
+                arrives(12 + slot, self.picked.at[slot])
+
+    def unpack(self, vec_out, ups, proj_bias, row, bias):
+        size = vec_out.shape[1] // 4
+        low = lambda a: a.astype(BF).astype(F32)
+        part = size // 4
+        for f in range(4):
+            vec_out[:, size * f : size * (f + 1)] = low(self.vec[f, :, 0:size])
+        proj_bias[...] = jnp.zeros_like(proj_bias)
+        for slot in range(2):
+            for f in range(4):
+                ups[slot : slot + 1, size * f : size * (f + 1)] = low(self.near[slot, f, 0:1, 0:size])
+                row[slot, 0:2, part * f : part * (f + 1)] = low(self.near[slot, f, 1:3, 0:part])
+            for i in range(3):
+                start = i * size
+                proj_bias[slot, :, start : start + 64] = row[slot, 0:1, 64 * i : 64 * i + 64]
+                proj_bias[slot, :, start + 128 : start + 192] = row[slot, 1:2, 64 * i : 64 * i + 64]
+        blocks, length = bias.shape[1], bias.shape[2]
+        spot = lax.broadcasted_iota(jnp.int32, (blocks, length), 0)
+        block = lax.broadcasted_iota(jnp.int32, (blocks, length), 1) // BLK
+        number = lambda mask: jnp.where(mask, 1.0, 0.0)
+        fixed = number(jnp.abs(spot - block) <= 1) + number(spot == 0) + number(spot == blocks - 1)
+        edge = jnp.logical_or(block == 0, block == blocks - 1)
+        spread_out = number(spot == block).astype(BF)
+        here = spot.astype(F32)
+        for slot in range(2):
+            ids = mm(self.picked[slot, :, 0:blocks].astype(BF), spread_out)
+            for i in range(3):
+                counts = fixed
+                for r in range(3):
+                    counts = counts + number(ids[3 * i + r : 3 * i + r + 1, :] == here)
+                counts = jnp.where(edge, 1.0, counts)
+                bias[3 * slot + i] = jnp.where(counts > 0.5, jnp.log(jnp.maximum(counts, 1.0)), -1e30)
+
+
+class Reduce:
+    def __init__(self, at, grads, work, plane, zline, final, send, recv, tall):
+        self.at, self.grads, self.work, self.plane, self.zline, self.final = at, grads, work, plane, zline, final
+        self.send, self.recv, self.tall = send, recv, tall
+
+    def cp(self, g, slot, kind, src, dst, device, recv_kind=None):
+        recv_kind = kind if recv_kind is None else recv_kind
+        return copy_to(src, dst, self.send.at[g, slot, kind], self.recv.at[g, slot, recv_kind], device)
+
+    def arrives(self, g, slot, kind, dst):
+        self.cp(g, slot, kind, dst, dst, self.at.core).wait_recv()
+
+    def plane_sends(self, g, slot):
+        at, grad, box = self.at, self.grads[g], self.plane.at[g, slot]
+        if g in self.tall:
+            two = pl.ds(at.other, 2)
+            return (
+                self.cp(g, slot, 0, grad.at[slot, two, 1 - at.c], box.at[0:2], at.ynbr),
+                self.cp(g, slot, 1, grad.at[slot, two, at.c], box.at[2:4], at.ynbr),
+            )
+        return (
+            self.cp(g, slot, 1, grad.at[slot, at.other, 1 - at.c], box.at[1], at.xnbr),
+            self.cp(g, slot, 3, grad.at[slot, at.other + 1, 1 - at.c], box.at[3], at.ynbr),
+            self.cp(g, slot, 0, grad.at[slot, at.pair, 1 - at.c], box.at[0], at.xnbr),
+            self.cp(g, slot, 2, grad.at[slot, at.other + 1, at.c], box.at[2], at.ynbr),
+        )
+
+    def sums(self, g, slot):
+        at, work, box = self.at, self.work.at[g, slot], self.plane.at[g, slot]
+        if g in self.tall:
+            return (self.cp(g, slot, 4, work.at[0:2], box.at[4:6], at.xnbr),)
+        return (
+            self.cp(g, slot, 4, work.at[0], box.at[4], at.ynbr),
+            self.cp(g, slot, 5, work.at[1], box.at[5], at.xnbr),
+        )
+
+    def plane0(self, g, slot):
+        for copy in self.plane_sends(g, slot):
+            copy.start()
+
+    def total(self, g, slot, i, piece, boxes):
+        came = sum(self.plane[g, slot, b].astype(F32) for b in boxes)
+        own = self.grads[g][slot, piece[0], piece[1]].astype(F32)
+        self.work[g, slot, i] = (own + came).astype(BF)
+
+    def plane1(self, g, slot):
+        at = self.at
+        copies = self.sums(g, slot)
+        if g in self.tall:
+            self.arrives(g, slot, 0, self.plane.at[g, slot, 0:2])
+            for i in range(2):
+                self.total(g, slot, i, (at.pair + i, 1 - at.c), (i,))
+            copies[0].start()
+            return
+        for i, kind, piece in ((0, 1, (at.other, at.c)), (1, 3, (at.pair + 1, 1 - at.c))):
+            self.arrives(g, slot, kind, self.plane.at[g, slot, kind])
+            self.total(g, slot, i, piece, (kind,))
+            copies[i].start()
+
+    def ours(self, g, slot):
+        return self.work.at[g, slot, pl.ds(2, 2)]
+
+    def down(self, g, slot):
+        return self.cp(g, slot, 6, self.ours(g, slot), self.zline.at[g, slot], self.at.zminus)
+
+    def upward(self, g, slot):
+        return self.cp(g, slot, 7, self.ours(g, slot), self.zline.at[g, 2], self.at.zplus)
+
+    def plane2(self, g, slot):
+        at = self.at
+        if g in self.tall:
+            self.arrives(g, slot, 1, self.plane.at[g, slot, 2:4])
+            self.arrives(g, slot, 4, self.plane.at[g, slot, 4:6])
+            boxes = ((2, 4), (3, 5))
+        else:
+            for kind in (0, 2, 4, 5):
+                self.arrives(g, slot, kind, self.plane.at[g, slot, kind])
+            boxes = ((0, 4), (2, 5))
+        for i in range(2):
+            self.total(g, slot, 2 + i, (at.pair + i, at.c), boxes[i])
+
+        @pl.when(at.p == 3)
+        def _():
+            self.down(g, slot).start()
+
+        if slot == 1:
+
+            @pl.when(at.p == 0)
+            def _():
+                self.upward(g, slot).start()
+
+    def add_line(self, g, slot, which):
+        box = 2 if which else slot
+        self.arrives(g, slot, 6 + which, self.zline.at[g, box])
+        for i in range(2):
+            self.work[g, slot, 2 + i] = (
+                self.work[g, slot, 2 + i].astype(F32) + self.zline[g, box, i].astype(F32)
+            ).astype(BF)
+
+    def line(self, g, slot, place):
+        at = self.at
+        if place < slot:
+            return
+
+        @pl.when(at.p == place)
+        def _():
+            self.add_line(g, slot, 0)
+            if slot == 1 and place == 1:
+                self.add_line(g, slot, 1)
+            if place > slot:
+                self.down(g, slot).start()
+            else:
+                self.hand_out(g, slot)
+
+    def hands(self, g, slot):
+        at, final = self.at, self.final[g]
+        mine = self.work.at[g, slot, 2 + at.k]
+        theirs = self.work.at[g, slot, 3 - at.k]
+        there = final.at[self.half(g, at.c)]
+        return (
+            self.cp(g, slot, 8, theirs, there, at.core, 8),
+            self.cp(g, slot, 9, mine, there, at.xnbr, 9),
+            self.cp(g, slot, 10, theirs, there, (at.core[0], 1 - at.c, at.t), 9),
+        )
+
+    def half(self, g, c):
+        n = self.final[g].shape[0] // 2
+        return pl.ds(pl.multiple_of(c * n, n), n)
+
+    def hand_out(self, g, slot):
+        at = self.at
+        for copy in self.hands(g, slot):
+            copy.start()
+        self.final[g][self.half(g, at.c), :] = self.work[g, slot, 2 + at.k]
+
+    def finish(self, g):
+        at, final = self.at, self.final[g]
+
+        @pl.when(at.k != at.own_core)
+        def _():
+            self.arrives(g, at.own_slot, 8, final.at[self.half(g, at.c)])
+
+        self.arrives(g, at.own_slot, 9, final.at[self.half(g, 1 - at.c)])
+        return final[...].astype(F32)
+
+    def sent(self, g):
+        at = self.at
+        for slot in range(2):
+            for copy in (*self.plane_sends(g, slot), *self.sums(g, slot)):
+                copy.wait_send()
+
+            @pl.when(at.p > slot)
+            def _():
+                self.down(g, slot).wait_send()
+
+            if slot == 1:
+
+                @pl.when(at.p == 0)
+                def _():
+                    self.upward(g, slot).wait_send()
+
+            @pl.when(at.p == slot)
+            def _():
+                for copy in self.hands(g, slot):
+                    copy.wait_send()
+
+
+def attend_back_chunk(h, q, key, query, value, key_t, bias, lse, upper, key_sum, value_sum, query_t):
+    cols = pl.ds(pl.multiple_of(q * QCHUNK, QCHUNK), QCHUNK)
+    some = query[h, cols, :]
+    upper = upper(cols)
+    scores = mm(key[h], some, NT)
+    length = scores.shape[0]
+    shift = bias[h, :, cols] - lse[h, :, cols]
+    scores = (scores.reshape(length // BLK, BLK, QCHUNK) + shift[:, None, :]).reshape(length, QCHUNK)
+    probs = jnp.exp(scores)
+    probs_grad = mm(value[h], upper, NT)
+    inner = jnp.sum(probs * probs_grad, axis=0, keepdims=True)
+    scores_grad = (probs * (probs_grad - inner)).astype(BF)
+    value_sum[...] += mm(probs.astype(BF), upper)
+    key_sum[...] += mm(scores_grad, some)
+    query_t[:, cols] = mm(key_t[...], scores_grad)
+
+
+def layer_kernel(
+    xs, cs, w_in, w_out, w_up, w_down, out_bias, norm_gain, norm_bias, up_bias, qv_bias, rand,
+    layer_blocks, grad_blocks, g_in, g_qv, g_out, g_outs, g_gains, g_shifts, g_up, g_ups, g_down,
+    x_all, up_half, low0, low1, low2, query, key, value, mixed, lse, bias, vectors, ups,
+    own, vec, near, ids, picked, proj_bias, bias_row,
+    grad0, grad_out, part_out, part_back, rows_f32, normed_one, inverse_one, first_b, second_b,
+    act, slope, flipped, grad_rows, key_t, key_sum, value_sum, query_t,
+    work, plane, zline, final0, final1, final2, small, small_out, sum_out, sum_in,
+    xs_send, xs_recv, xc_send, xc_recv, cs_send, cs_recv, p_send, p_recv, v_send, v_recv,
+    lo_send, lo_recv, gi_send, gi_recv, w_send, w_recv, send, recv, row_send, row_recv, small_send, small_recv,
+):
+    at = Place()
+    letters = Vectors(at, own, vec, near, ids, picked, (v_send, v_recv))
+    finals = (final0, final1, final2)
+    wide = w_in.shape[2]
+
+    def pack():
+        for h in range(3):
+            final0[:, h * wide : (h + 1) * wide] = w_in[h].astype(BF)
+        final0[:, 3 * wide : 4 * wide] = w_out[...].T.astype(BF)
+        final1[...] = w_up[...].astype(BF)
+        final2[...] = w_down[...].astype(BF)
+        own[...] = jnp.zeros_like(own)
+        ids[...] = jnp.zeros_like(ids)
+        vec[at.f] = jnp.zeros(vec.shape[1:], F32)
+        letters.fill(out_bias, norm_gain, norm_bias, up_bias, qv_bias, rand)
+
+    greet(at, pack)
+    gather = Gather(at, finals, (low0, low1, low2), p_send, p_recv, tall=(0,))
+    tokens = Swap(at, xs, x_all, 512, xs_send, xs_recv)
+    upstreams = Swap(at, cs, up_half, 0, cs_send, cs_recv)
+    part = xs.shape[1]
+    width = x_all.shape[1]
+    letters.start()
+    tokens.start_in()
+    for g in range(3):
+        gather.own(g)
+    gather.step_z(0, 0)
+    gather.step_z(0, 1)
+    gather.step_relay(0, 0)
+    gather.step_relay(0, 1)
+
+    def to_core(s, half):
+        rows = x_all.at[pl.ds(pl.multiple_of(half * 512 + s * part, part), part)]
+        return copy_to(rows, rows, xc_send.at[s], xc_recv.at[s], at.core)
+
+    for s in range(4):
+        tokens.wait_in(s)
+        to_core(s, at.k).start()
+    gather.step_z(1, 0)
+    gather.step_z(1, 1)
+    upstreams.start_in()
+    letters.wait()
+    letters.unpack(vectors, ups, proj_bias, bias_row, bias)
+    small[...] = jnp.zeros_like(small)
+    for s in range(4):
+        to_core(s, 1 - at.k).wait_recv()
+    gather.step_last(0)
+
+    dim = query.shape[2]
+    for slot in range(2):
+
+        @pl.loop(0, 4)
+        def _(r):
+            rows = pl.ds(pl.multiple_of(r * 256, 256), 256)
+            weight = low0[slot, :, :, :, 0:640].reshape(width, 640)
+            got = mm(x_all[rows, :], weight) + proj_bias[slot]
+            for i in range(3):
+                h = slot * 3 + i
+                start = i * 3 * dim
+                query[h, rows, :] = (got[:, start : start + dim] * dim**-0.5).astype(BF)
+                key[h, rows, :] = got[:, start + dim : start + 2 * dim].astype(BF)
+                one = got[:, start + 2 * dim : start + 3 * dim]
+                value[h, rows, :] = one.astype(BF)
+                flipped[384 + h * dim : 384 + (h + 1) * dim, rows] = one.T.astype(BF)
+
+        if slot == 0:
+            gather.step_relay(1, 0)
+            gather.step_relay(1, 1)
+    gather.step_z(2, 0)
+    gather.step_z(2, 1)
+
+    def attend_forward(low_head, high_head):
+        @pl.loop(low_head, high_head)
+        def _(h):
+            @pl.loop(0, 1024 // QCHUNK)
+            def _(q):
+                spot = pl.ds(pl.multiple_of(h * dim, dim), dim)
+                value_t = flipped.at[pl.ds(pl.multiple_of(384 + h * dim, dim), dim)]
+                attend_chunk(h, q, key, query, value_t, bias, lse, flipped.at[spot])
+
+    attend_forward(0, 3)
+    gather.step_relay(2, 0)
+    gather.step_relay(2, 1)
+    attend_forward(3, 6)
+
+    @pl.loop(0, 4)
+    def _(r):
+        rows = pl.ds(pl.multiple_of(r * 256, 256), 256)
+        blank = jnp.zeros((dim, 256), BF)
+        for slot in range(2):
+            heads = jnp.concatenate([blank, flipped[slot * 192 : slot * 192 + 192, rows]], axis=0)
+            mixed[rows, slot * 256 : slot * 256 + 256] = heads.T
+
+    layer = Swap(at, layer_blocks, up_half, 0, lo_send, lo_recv)
+    inputs = Swap(at, grad_blocks, grad_rows, 0, gi_send, gi_recv)
+    reduce = Reduce(at, (grad0, low1, low2), work, plane, zline, finals, w_send, w_recv, tall=(0, 2))
+    cores = Cores(at, part_out, part_back, send, recv, row_send, row_recv)
+    square = lambda full, slot: full[slot].reshape(width, width)
+    out_part = lambda slot: low0[slot, :, :, :, 512:768].reshape(width, 256)
+    local = lambda i: pl.ds(pl.multiple_of(i * ROWS, ROWS), ROWS)
+
+    def tally(row, value):
+        small[row : row + 1, :] += row_sum(value)
+
+    def branch_part(rows):
+        return mm(mixed[rows, 0:256], out_part(0), NT) + mm(mixed[rows, 256:512], out_part(1), NT)
+
+    def branch_done(i, rows, total):
+        normed, inverse = norm_stats(x_all[rows, :].astype(F32) + (total + vectors[0:1, :]))
+        value = normed * vectors[2:3, :] + vectors[4:5, :]
+        normed_one[local(i), :] = normed
+        inverse_one[local(i), :] = inverse
+        rows_f32[local(i), :] = value
+        first_b[rows, :] = value.astype(BF)
+        cores.row(0, first_b, at.k, i).start()
+
+    cores.reduce(0, branch_part, branch_done)
+
+    def up(rows):
+        for slot in range(2):
+            inner = mm(first_b[rows, :], square(low1, slot)) + ups[slot : slot + 1, :]
+            value, slope_value = gelu_both(inner)
+            act[slot, rows, :] = value.astype(BF)
+            slope[slot, rows, :] = slope_value.astype(BF)
+
+    gather.sent(0)
+    gather.step_last(1)
+    gather.sent(1)
+    cores.over_rows(0, first_b, up)
+    gather.step_last(2)
+    gather.sent(2)
+    for s in range(4):
+        upstreams.wait_in(s)
+
+    def second_part(rows):
+        return mm(act[0, rows, :], square(low2, 0), NT) + mm(act[1, rows, :], square(low2, 1), NT)
+
+    def second_done(i, rows, total):
+        normed, inverse = norm_stats(rows_f32[local(i), :] + (total + vectors[1:2, :]))
+        layer_row = (normed * vectors[3:4, :] + vectors[5:6, :]).astype(BF)
+        upstream = up_half[local(i), :].astype(F32)
+        up_half[local(i), :] = layer_row
+        scaled = upstream * vectors[3:4, :]
+        grad = inverse * (
+            scaled
+            - jnp.mean(scaled, axis=-1, keepdims=True)
+            - normed * jnp.mean(scaled * normed, axis=-1, keepdims=True)
+        )
+        rows_f32[local(i), :] = grad
+        low = grad.astype(BF)
+        second_b[rows, :] = low
+        cores.row(1, second_b, at.k, i).start()
+        tally(1, low.astype(F32))
+        tally(3, upstream * normed)
+        tally(5, upstream)
+
+    cores.reduce(1, second_part, second_done)
+    for s in range(4):
+        layer.start_out(s)
+
+    def down(rows):
+        for slot in range(2):
+            grad = mm(second_b[rows, :], square(low2, slot)) * slope[slot, rows, :].astype(F32)
+            low = grad.astype(BF)
+            slope[slot, rows, :] = low
+            tally(6 + slot, low.astype(F32))
+
+    cores.over_rows(1, second_b, down)
+    flip(flipped, second_b)
+    for slot in range(2):
+        product(low2, slot, flipped, lambda: act[slot])
+        reduce.plane0(2, slot)
+
+    def first_part(rows):
+        return mm(slope[0, rows, :], square(low1, 0), NT) + mm(slope[1, rows, :], square(low1, 1), NT)
+
+    def first_done(i, rows, total):
+        grad = total + rows_f32[local(i), :]
+        normed = normed_one[local(i), :]
+        tally(2, grad * normed)
+        tally(4, grad)
+        scaled = grad * vectors[2:3, :]
+        back = inverse_one[local(i), :] * (
+            scaled
+            - jnp.mean(scaled, axis=-1, keepdims=True)
+            - normed * jnp.mean(scaled * normed, axis=-1, keepdims=True)
+        )
+        rows_f32[local(i), :] = back
+        low = back.astype(BF)
+        second_b[rows, :] = low
+        cores.row(2, second_b, at.k, i).start()
+        tally(0, low.astype(F32))
+
+    cores.reduce(2, first_part, first_done)
+    flip(flipped, first_b)
+    for slot in range(2):
+        product(low1, slot, flipped, lambda: slope[slot])
+        reduce.plane0(1, slot)
+
+    mixed_grad = first_b
+
+    def mix_back(rows):
+        for slot in range(2):
+            mixed_grad[rows, slot * 256 : slot * 256 + 256] = mm(second_b[rows, :], out_part(slot)).astype(BF)
+
+    cores.over_rows(2, second_b, mix_back)
+    flip(flipped, second_b)
+
+    @pl.loop(0, 4)
+    def _(r):
+        rows = pl.ds(pl.multiple_of(r * 192, 192), 192)
+        grad_out[rows, :] = mm(flipped[rows, :], mixed[...]).astype(BF)
+
+    flip(flipped, x_all)
+    proj_grad = act
+    for slot in range(2):
+        proj_grad[slot, :, 576:640] = jnp.zeros((1024, 64), BF)
+
+    def attend(h, part):
+        if part == 0:
+            key_t[...] = key[h].astype(F32).T.astype(BF)
+            key_sum[...] = jnp.zeros_like(key_sum)
+            value_sum[...] = jnp.zeros_like(value_sum)
+
+        @pl.loop(part * 2, part * 2 + 2)
+        def _(q):
+            column = (h // 3) * 256 + (h % 3 + 1) * 64
+            attend_back_chunk(
+                h, q, key, query, value, key_t, bias, lse,
+                lambda cols: mixed_grad[cols, column : column + 64], key_sum, value_sum, query_t,
+            )
+
+        if part == 1:
+            start = (h % 3) * 192
+            proj_grad[h // 3, :, start : start + 64] = (query_t[...] * 0.125).T.astype(BF)
+            proj_grad[h // 3, :, start + 64 : start + 128] = key_sum[...].astype(BF)
+            proj_grad[h // 3, :, start + 128 : start + 192] = value_sum[...].astype(BF)
+
+    def in_grads(slot):
+        @pl.loop(0, 4)
+        def _(r):
+            rows = pl.ds(pl.multiple_of(r * 192, 192), 192)
+            got = mm(flipped[rows, :], proj_grad[slot, :, 0:640])
+            out_part = grad_out[rows, slot * 256 : slot * 256 + 256]
+            grad0[slot, r, :, :, 0:512] = got[:, 0:512].astype(BF).reshape(2, 96, 512)
+            shared = got[:, 512:640] + out_part[:, 0:128].astype(F32)
+            grad0[slot, r, :, :, 512:640] = shared.astype(BF).reshape(2, 96, 128)
+            grad0[slot, r, :, :, 640:768] = out_part[:, 128:256].reshape(2, 96, 128)
+
+        reduce.plane0(0, slot)
+
+    def both(step, g, *more):
+        for slot in range(2):
+            step(g, slot, *more)
+
+    attend(0, 0)
+    both(reduce.plane1, 2)
+    attend(0, 1)
+    attend(1, 0)
+    both(reduce.plane2, 2)
+    attend(1, 1)
+    both(reduce.line, 2, 2)
+    attend(2, 0)
+    both(reduce.plane1, 1)
+    both(reduce.line, 2, 1)
+    attend(2, 1)
+    both(reduce.line, 2, 0)
+    in_grads(0)
+    attend(3, 0)
+    both(reduce.plane2, 1)
+    attend(3, 1)
+    both(reduce.line, 1, 2)
+    attend(4, 0)
+    both(reduce.line, 1, 1)
+    reduce.plane1(0, 0)
+    attend(4, 1)
+    both(reduce.line, 1, 0)
+    attend(5, 0)
+    reduce.plane2(0, 0)
+    attend(5, 1)
+    in_grads(1)
+    reduce.line(0, 0, 2)
+
+    def in_part(rows):
+        return sum(
+            mm(proj_grad[slot, rows, 0:640], low0[slot, :, :, :, 0:640].reshape(width, 640), NT)
+            for slot in range(2)
+        )
+
+    def in_done(i, rows, total):
+        grad_rows[local(i), :] = (total + rows_f32[local(i), :]).astype(BF)
+        for s in range(ROWS // 128):
+            inputs.start_out(i * (ROWS // 128) + s)
+
+    cores.reduce(3, in_part, in_done)
+
+    t = at.t
+    steps = (at.xnbr, at.ynbr, (at.f, at.c, t + 1 - 2 * lax.rem(t, 2)), (at.f, at.c, lax.rem(t + 2, 4)))
+    hops = [
+        copy_to(sum_out.at[i], sum_in.at[i], small_send.at[i], small_recv.at[i], device)
+        for i, device in enumerate(steps)
+    ]
+
+    def small_next(i):
+        hops[i].wait_recv()
+        if i < 3:
+            sum_out[i + 1] = sum_out[i] + sum_in[i]
+            hops[i + 1].start()
+        else:
+            small_out[at.k] = sum_out[i] + sum_in[i]
+
+    sum_out[0] = small[...]
+    for slot in range(2):
+        sum_out[0, 8 + slot : 9 + slot, 0:640] = row_sum(proj_grad[slot, :, 0:640].astype(F32))
+    hops[0].start()
+    reduce.line(0, 0, 1)
+    reduce.plane1(0, 1)
+    small_next(0)
+    reduce.line(0, 0, 0)
+    small_next(1)
+    reduce.plane2(0, 1)
+    small_next(2)
+    reduce.line(0, 1, 2)
+    small_next(3)
+    mine = small_out.at[at.k]
+    both_cores = copy_to(mine, mine, small_send.at[4], small_recv.at[4], at.core)
+    both_cores.start()
+    reduce.line(0, 1, 1)
+    for copy in hops:
+        copy.wait_send()
+    g_down[...] = reduce.finish(2)
+    g_up[...] = reduce.finish(1)
+    got = reduce.finish(0)
+    fr = g_up.shape[0]
+    for h in range(3):
+        g_in[h] = got[:, h * fr : (h + 1) * fr]
+    g_out[...] = got[:, 3 * fr : 4 * fr].T
+    both_cores.wait_send()
+    copy_to(small_out.at[1 - at.k], small_out.at[1 - at.k], small_send.at[4], small_recv.at[4], at.core).wait_recv()
+    sums = small_out[0, 0:8, :] + small_out[1, 0:8, :]
+    used = small_out.at[at.own_core]
+    up_row = used[pl.ds(6 + at.own_slot, 1), :]
+    proj_row = used[pl.ds(8 + at.own_slot, 1), :]
+    pick = lambda j: jnp.concatenate(
+        [proj_row[:, i * fr + 64 * j : i * fr + 64 * j + 64] for i in range(3)], axis=1
+    )
+    pair_rows = jnp.concatenate([pick(0), pick(2)], axis=0)
+    quarter = fr // 4
+    for f in range(4):
+
+        @pl.when(at.f == f)
+        def _():
+            piece = sums[:, f * fr : (f + 1) * fr]
+            g_outs[...] = piece[0:2]
+            g_gains[...] = piece[2:4]
+            g_shifts[...] = piece[4:6]
+            g_ups[...] = up_row[:, f * fr : (f + 1) * fr]
+            g_qv[...] = pair_rows[:, f * quarter : (f + 1) * quarter]
+
+    for s in range(4):
+        layer.wait_out(s)
+        inputs.wait_out(s)
+    layer.sent(True)
+    inputs.sent(True)
+    for g in range(3):
+        reduce.sent(g)
+    letters.sent()
+    tokens.sent()
+    upstreams.sent()
+    for s in range(4):
+        to_core(s, at.k).wait_send()
+
+
+def layer_call(xs, cs, w_in, w_out, w_up, w_down, out_bias, norm_gain, norm_bias, up_bias, qv_bias, rand):
+    width = xs.shape[2]
+    length, half = 1024, 512
+    heads, dim = 6, 64
+    blocks = length // BLK
+    parts = half // ROWS
+    fr = width // 4
+    piece = (fr // 2, width)
+    shape = jax.ShapeDtypeStruct
+    dma = lambda *dims: pltpu.SemaphoreType.DMA(dims)
+    low = lambda *dims: pltpu.VMEM(dims, BF)
+    full = lambda *dims: pltpu.VMEM(dims, F32)
+    anywhere = pl.BlockSpec(memory_space=pl.ANY)
+    return pl.pallas_call(
+        layer_kernel,
+        out_shape=(
+            shape(xs.shape, BF),
+            shape(xs.shape, BF),
+            shape((3, fr, fr), F32),
+            shape((2, fr // 4), F32),
+            shape((fr, fr), F32),
+            shape((2, fr), F32),
+            shape((2, fr), F32),
+            shape((2, fr), F32),
+            shape((fr, width), F32),
+            shape((1, fr), F32),
+            shape((fr, width), F32),
+        ),
+        in_specs=[anywhere] * 2 + [vmem()] * 10,
+        out_specs=[anywhere] * 2 + [vmem()] * 9,
+        scratch_shapes=[
+            low(length, width),
+            low(half, width),
+            low(2, 4, 2, *piece),
+            low(2, 4, 2, *piece),
+            low(2, 4, 2, *piece),
+            low(heads, length, dim),
+            low(heads, length, dim),
+            low(heads, length, dim),
+            low(length, 512),
+            full(heads, 1, length),
+            full(heads, blocks, length),
+            full(8, width),
+            full(2, width),
+            full(8, 256),
+            full(4, 8, 256),
+            full(2, 4, 8, 256),
+            full(4, 16, 128),
+            full(2, 16, 128),
+            full(2, 1, 640),
+            full(2, 8, 256),
+            low(2, 4, 2, *piece),
+            low(width, 512),
+            full(parts, ROWS, width),
+            full(parts, ROWS, width),
+            full(half, width),
+            full(half, width),
+            full(half, 1),
+            low(length, width),
+            low(length, width),
+            low(2, length, width),
+            low(2, length, width),
+            low(width, length),
+            low(half, width),
+            low(dim, length),
+            full(length, dim),
+            full(length, dim),
+            full(dim, length),
+            low(3, 2, 4, *piece),
+            low(3, 2, 6, *piece),
+            low(3, 3, 2, *piece),
+            low(fr, width),
+            low(fr, width),
+            low(fr, width),
+            full(16, width),
+            full(2, 16, width),
+            full(4, 16, width),
+            full(4, 16, width),
+            dma(4),
+            dma(4),
+            dma(4),
+            dma(4),
+            dma(4),
+            dma(4),
+            dma(3, 2, 7),
+            dma(3, 2, 7),
+            dma(15),
+            dma(14),
+            dma(4),
+            dma(4),
+            dma(4),
+            dma(4),
+            dma(3, 2, 11),
+            dma(3, 2, 11),
+            dma(4, parts),
+            dma(4, parts),
+            dma(3, parts),
+            dma(3, parts),
+            dma(5),
+            dma(5),
+        ],
+        compiler_params=pltpu.CompilerParams(
+            collective_id=1, has_side_effects=True, vmem_limit_bytes=VMEM_LIMIT
+        ),
+        name="layer",
+    )(xs, cs, w_in, w_out, w_up, w_down, out_bias, norm_gain, norm_bias, up_bias, qv_bias, rand)
+
+
+def sequence_shards(hidden_in, rand_blocks, w_in, qv_bias, w_out, out_bias, norm_gain, norm_bias, w_up, up_bias, w_down, cotangent):
+    layer_blocks, grad_blocks, *grads = layer_call(
+        hidden_in.transpose(1, 0, 2),
+        cotangent.transpose(1, 0, 2),
+        w_in.transpose(1, 0, 2),
+        w_out,
+        w_up,
+        w_down.T,
+        out_bias,
+        norm_gain,
+        norm_bias,
+        up_bias[None],
+        qv_bias,
+        rand_blocks.transpose(2, 3, 0, 1),
+    )
+    grads[0] = grads[0].transpose(1, 0, 2)
+    grads[7] = grads[7][0]
+    grads[8] = grads[8].T
+    return (layer_blocks.transpose(1, 0, 2), grad_blocks.transpose(1, 0, 2), *grads)
+
+
 def solution(mesh):
     placed = (
         P(("ctx", "tp"), "fsdp", None),
@@ -539,8 +1713,17 @@
         P("tp", "fsdp"),
         P(("ctx", "tp"), "fsdp", None),
     )
+    sizes = tuple(mesh.shape[a] for a in ("fsdp", "ctx", "tp"))
+
+    def local(*args):
+        part_rows, seqs, width = args[0].shape
+        rows, heads, wide = args[2].shape
+        whole = sizes == (4, 2, 4) and (part_rows, seqs, width) == (128, 4, 768)
+        whole = whole and (rows, heads, wide) == (192, 3, 192) and args[8].shape == (192, 768)
+        return (sequence_shards if whole else span_shards)(*args)
+
     return jax.shard_map(
-        shards,
+        local,
         mesh=mesh,
         in_specs=placed,
         out_specs=(

time: 1880 us -> 254 us (0.14)
  waiting for transfers between devices: 955 us -> 0 us
  local copies, waits for them, and re-layouts: 360 us -> 13.1 us
  Pallas kernels: 0 us -> 240 us
  blocking collectives: 180 us -> 0 us
  matrix products: 172 us -> 0 us
  other arithmetic: 164 us -> 0 us
    reduce_scatter x7 -> x0, waiting for transfers between devices: 503 us -> none  [the longest x4 418 us: rows_sum(): lax.psum_scatter(lax.dot_general(left, right, (((1,), (contract,)), ((),...]
    pallas_call x0 -> x1, Pallas kernels: none -> 240 us  [layer_call(): pl.pallas_call(layer_kernel, out_shape=(shape(xs.shape, BF), shape(xs.sha...]
    all_gather x6 -> x0, waiting for transfers between devices: 222 us -> none  [the longest x4 206 us: rows_all(): return lax.all_gather(value, 'tp', axis=0, tiled=True)]
    dot_general x46 -> x0, matrix products: 168 us -> none  [the longest x4 22.9 us: rows_sum(): lax.dot_general(left, right, (((1,), (contract,)), ((), ())), preferred_e...]
    psum x5 -> x0, waiting for transfers between devices: 144 us -> none  [the longest x1 60.5 us: shards(): lax.psum((shares[0], shares[1], shares[2], shares[6], shares[7], shares[8...]
    all_gather x16 -> x0, blocking collectives: 130 us -> none  [the longest x8 75 us: random_pairs_for(): whole = lax.all_gather(block_group, 'ctx', axis=2, tiled=True)]
    concatenate x44 -> x0, local copies, waits for them, and re-layouts: 77.7 us -> none  [the longest x12 48.8 us: attend_back(): pairs_grad = jnp.concatenate([keys_grad, values_grad], axis=-1)]
    scatter-add x18 -> x0, other arithmetic: 76.3 us -> none  [the longest x4 53.1 us: random_back(): spread_grad = jnp.zeros((group, heads, blocks_all, BLK, pair_width), jnp....]
  transfers between devices with their start and end apart: 31 -> 0, of which waited for: 26 -> 0; matrix products, arithmetic and copies ran while one was open for 12% -> 0% of each run, Pallas kernels for 0% -> 0%
where the time goes in v3:
time: 254 us
  Pallas kernels  240 us (94%)
  local copies, waits for them, and re-layouts  13.1 us (5%)
    pallas_call x1, Pallas kernels, layer_call(): pl.pallas_call(layer_kernel, out_shape=(shape(xs.shape, BF), shape(xs.sha...  240 us
    unnamed x31, local copies, waits for them, and re-layouts  10.4 us

profile of v3, /device:TPU:11, one launch (start us, length us, event | category | flops | bytes accessed | tf_op | source)
XLA Modules:
  0.0 253.6 jit_solution(10029956722497733301)
XLA Ops:
  0.6 2.7 %copy_bitcast_fusion = (bf16[4,128,768]{2,1,0:T(8,128)(2,1)}, bf16[4,128,768]{2,1,0:T(8,128)(2,1)}) fusion(bf16[128,4,768]{2,1,0:T(4,128)(2,1)} %param.23, bf16[128,4,768]{2,1,0:T(4,128)(2,1)} %param.12), kind=kLoop, calls=%fused_computation | loop fusion | bytes 3145728 | tf_op jit(solution)/shard_map/transpose | solution.py:1683
  3.4 239.8 %layer.1 = (bf16[4,128,768]{2,1,0:T(8,128)(2,1)}, bf16[4,128,768]{2,1,0:T(8,128)(2,1)}, f32[3,192,192]{2,1,0:T(8,128)}, f32[2,48]{1,0:T(2,128)}, f32[192,192]{1,...) custom-call(bf16[4,128,768]{2,1,0:T(8,128)(2,1)} %get-tuple-element., ...), custom_call_target="tpu_custom_call" | custom-call | tf_op jit(solution)/shard_map/layer/pallas_call | solution.py:1585
  243.2 0.0 copy-start
  243.2 2.7 %copy.25 = bf16[128,4,768]{2,1,0:T(4,128)(2,1)} copy(bf16[128,4,768]{2,0,1:T(8,128)(2,1)} %bitcast.14) | data formatting | bytes 1572864
  245.9 0.0 copy-done
  245.9 1.5 copy.26
  247.4 0.0 copy-done.3
  247.4 0.8 copy.38
  248.2 0.0 copy-done.9
  248.2 0.6 copy.39
  248.8 0.0 copy-done.4
  248.8 0.7 copy.40
  249.5 0.0 copy-done.7
  249.5 0.6 copy.41
  250.1 0.1 copy-done.6
  250.2 0.6 copy.42
  250.7 0.1 copy-done.5
  250.8 0.6 copy.43
  251.4 0.0 copy-done.2
  251.4 0.8 copy.44
  252.2 0.0 copy-done.8
  252.2 0.6 copy.45
  252.8 0.0 copy-done.1
  252.8 0.8 copy.46
  (9 shorter events, 0.0 us)
Async XLA Ops:
  243.2 2.7 %copy-start = (bf16[4,128,768]{2,1,0:T(8,128)(2,1)S(1)}, bf16[4,128,768]{2,1,0:T(8,128)(2,1)}, u32[]{:S(2)}) copy-start(bf16[4,128,768]{2,1,0:T(8,128)(2,1)} %get-tuple-element.23) | copy-start | bytes 2359300
  245.9 1.5 copy-start.3
  247.4 0.8 copy-start.9
  247.4 1.4 copy-start.4
  247.4 4.0 %copy-start.2 = (f32[192,768]{1,0:T(8,128)S(1)}, f32[192,768]{1,0:T(8,128)}, u32[]{:S(2)}) copy-start(f32[192,768]{1,0:T(8,128)} %get-tuple-element.65) | copy-start | bytes 1769476
  248.8 0.7 copy-start.7
  249.5 0.7 copy-start.6
  250.2 0.7 copy-start.5
  251.4 0.8 copy-start.8
  251.4 1.4 copy-start.1
